TPU v7x, 128 devices: a whole 4x4x4 slice. The times are simulated.
128 devices in a mesh: head: 4 (over y), seq: 32 (over z, x, core).
Axes of the slice: x: 4, y: 4, z: 4, core: 2. Of those that a mesh axis runs over, the one named last changes fastest.
Arguments:
- inputs: bfloat16 [32768, 4096], P(('seq', 'head')), may hold values from -6 to 6
- dt_raw: bfloat16 [32768, 64], P(('seq', 'head')), may hold values from -4 to 4
- b_proj: bfloat16 [32768, 128], P(('seq', 'head')), may hold values from -0.59765625 to 0.59765625
- c_proj: bfloat16 [32768, 128], P(('seq', 'head')), may hold values from -0.59765625 to 0.59765625
- a_log: float32 [64], P('head'), may hold values from -12 to -2
- d_skip: float32 [64], P('head'), may hold values from 0.5 to 1.5
- seg_ids: int32 [32768], P('seq'), may hold values from 0 to 7, as said below
- cotangent: bfloat16 [32768, 4096], P(('seq', 'head')), may hold values from -6 to 6
Outputs:
- mixer_out: bfloat16 [32768, 4096], P(('seq', 'head'))
- grad_inputs: bfloat16 [32768, 4096], P(('seq', 'head'))
- grad_dt_raw: bfloat16 [32768, 64], P(('seq', 'head'))
- grad_b: float32 [32768, 128], P(('seq', 'head'))
- grad_c: float32 [32768, 128], P(('seq', 'head'))
- grad_a_log: float32 [64], P('head')
- grad_d_skip: float32 [64], P('head')
Inputs may be any that keep to these rules, and one draw needn't show every extreme that they name: `seg_ids`: segment numbers never fall along the ordering and each is used; each segment is a contiguous run of at most 8192 tokens; segment 0 ends within the first 512 tokens and segment 1 has exactly 8192 tokens.
All inputs are finite; a program needn't handle non-finite values.
Results may differ from a plain program's by a relative error of at most 0.018.
Values may be sent and summed in bfloat16 or wider, within the bound.
No kernel may reach another device: no remote copies, remote signals or barrier semaphores. Data moves between devices by JAX's collectives and lax.ppermute only.
A program may use at most 256 MiB of HBM per device.

v0:
```python
import jax
import jax.numpy as jnp
from jax import lax
from jax.experimental import pallas as pl
from jax.experimental.pallas import tpu as pltpu
from jax.sharding import PartitionSpec as P

HEADS = 64
DIM = 64
STATE = 128
BLOCK = 256
WIDTH = HEADS * DIM
PARTS = 128
PIECE = STATE * WIDTH // (PARTS * 128)
ROWS = STATE // PIECE
CARRY = 2 * PIECE
META = 8
LOG2E = 1.4426950408889634
F32 = jnp.float32
BF16 = jnp.bfloat16


def dot(a, b):
    return jnp.dot(a, b, preferred_element_type=F32)


def dot_nt(a, b):
    return lax.dot_general(a, b, (((1,), (1,)), ((), ())), preferred_element_type=F32)


def dot_tn(a, b):
    return lax.dot_general(a, b, (((0,), (0,)), ((), ())), preferred_element_type=F32)


def iota(shape, axis):
    return lax.broadcasted_iota(jnp.int32, shape, axis)


def ones_where(mask):
    return jnp.where(mask, 1.0, 0.0).astype(BF16)


def split2(value):
    high = value.astype(BF16)
    return high, (value - high.astype(F32)).astype(BF16)


def split3(value):
    high = value.astype(BF16)
    return (high,) + split2(value - high.astype(F32))


def spread(head0, lanes):
    shape = (2 * HEADS, lanes)
    return ones_where((iota(shape, 0) & (HEADS - 1)) == (iota(shape, 1) >> 6) + head0)


def gather_heads(head0, lanes, period):
    shape = (lanes, HEADS)
    return ones_where(((iota(shape, 0) & (period - 1)) >> 6) + head0 == iota(shape, 1))


def whole(*shape):
    return pl.BlockSpec(shape, lambda *_: (0,) * len(shape))


def wide(lanes):
    return pl.BlockSpec((BLOCK, lanes), lambda i: (0, i))


def pieces(lanes, rows):
    return pl.BlockSpec((PARTS * lanes // WIDTH, rows, 128), lambda i: (i, 0, 0))


def params(mib=24):
    return pltpu.CompilerParams(vmem_limit_bytes=mib * 1024 * 1024)


def cost(flops, moved, exps):
    return pl.CostEstimate(flops=flops, bytes_accessed=moved, transcendentals=exps)


def like(shape, kind=F32):
    return jax.ShapeDtypeStruct(shape, kind)


STATES_LANES = 1024


def states_kernel(
    place_ref, raw_ref, gains_ref, seg_ref, x_ref, g_ref, b_ref, c_ref,
    pay_ref, scal_ref, cum2_ref, half_ref, rate_ref, row_ref,
    bt_ref, ct_ref, meta_ref,
):
    step = pl.program_id(0)

    @pl.when(step == 0)
    def _():
        raw = raw_ref[...].astype(F32)
        dt = jnp.maximum(raw, 0.0) + jnp.log1p(jnp.exp(-jnp.abs(raw)))
        square = (BLOCK, BLOCK)
        upto = ones_where(iota(square, 0) <= iota(square, 1))
        high, mid, low = split3(dt)
        sums = dot(high, upto) + dot(mid, upto) + dot(low, upto)
        gains = gains_ref[...]
        alog = jnp.concatenate([gains[k : k + 1] for k in range(0, gains.shape[0], 2)], axis=1)
        rate = jnp.exp(jnp.broadcast_to(alog, (128, HEADS)).T)
        cum = -rate[:, :1] * sums
        tot = cum[:, BLOCK - 1 :]
        block = 2 * (place_ref[0] % (seg_ref.shape[0] // 2))
        seg = jnp.concatenate(
            [seg_ref[pl.ds(block, 1), :], seg_ref[pl.ds(block + 1, 1), :]], axis=1
        ).astype(F32)
        first, last = seg[:, :1], seg[:, BLOCK - 1 :]
        end = jnp.where(seg == last, jnp.exp(tot - cum), 0.0)
        start = jnp.where(seg == first, jnp.exp(cum), 0.0)
        weight = end * dt
        scal_ref[0] = end
        scal_ref[1] = weight
        scal_ref[2] = start
        scal_ref[3] = dt
        cum2_ref[...] = cum * LOG2E
        half_ref[0] = jnp.concatenate(split2(weight), axis=0).T
        half_ref[1] = jnp.concatenate(split2(start), axis=0).T
        half_ref[2] = jnp.concatenate(split2(dt), axis=0).T
        rate_ref[...] = rate
        row_ref[...] = seg
        bt_ref[...] = b_ref[...].T
        ct_ref[...] = c_ref[...].T
        kind = iota((HEADS, 128), 1)
        columns = jnp.zeros((HEADS, 128), F32)
        for k, part in enumerate(split3(tot)):
            columns = jnp.where(kind == k, part.astype(F32), columns)
        columns = jnp.where(kind == 3, first, jnp.where(kind == 4, last, columns))
        rows = jnp.concatenate([columns, jnp.zeros((HEADS, 128), F32)], axis=0).T
        meta_ref[...] = rows[:16].astype(BF16)

    copy = spread(step * (STATES_LANES // DIM), STATES_LANES)
    meta = dot(meta_ref[...], copy)[:META].astype(BF16)
    x_weighted = (x_ref[...].astype(F32) * dot(half_ref[0], copy)).astype(BF16)
    contrib = dot(bt_ref[...], x_weighted).astype(BF16)
    g_scaled = (g_ref[...].astype(F32) * dot(half_ref[1], copy)).astype(BF16)
    dh_low = dot(ct_ref[...], g_scaled).astype(BF16)
    for j in range(STATES_LANES // 128):
        lanes = slice(j * 128, (j + 1) * 128)
        for r in range(ROWS):
            rows = slice(r * PIECE, (r + 1) * PIECE)
            pay_ref[j * ROWS + r, :PIECE, :] = contrib[rows, lanes]
            pay_ref[j * ROWS + r, PIECE:CARRY, :] = dh_low[rows, lanes]
            pay_ref[j * ROWS + r, CARRY:, :] = meta[:, lanes]


def states(place, raw_t, gains, seg_ids, x, g, b, c):
    return pl.pallas_call(
        states_kernel,
        grid=(WIDTH // STATES_LANES,),
        in_specs=[
            pl.BlockSpec(memory_space=pltpu.SMEM),
            whole(HEADS, BLOCK), whole(*gains.shape), whole(*seg_ids.shape),
            wide(STATES_LANES), wide(STATES_LANES), whole(BLOCK, STATE), whole(BLOCK, STATE),
        ],
        out_specs=[
            pieces(STATES_LANES, CARRY + META), whole(4, HEADS, BLOCK), whole(HEADS, BLOCK),
            whole(3, BLOCK, 2 * HEADS), whole(HEADS, 128), whole(1, BLOCK),
        ],
        out_shape=[
            like((PARTS, CARRY + META, 128), BF16), like((4, HEADS, BLOCK)), like((HEADS, BLOCK)),
            like((3, BLOCK, 2 * HEADS), BF16), like((HEADS, 128)), like((1, BLOCK)),
        ],
        scratch_shapes=[
            pltpu.VMEM((STATE, BLOCK), BF16),
            pltpu.VMEM((STATE, BLOCK), BF16),
            pltpu.VMEM((16, 2 * HEADS), BF16),
        ],
        compiler_params=params(),
        cost_estimate=cost(10**9, 8 * 10**6, 10**5),
        name="states",
    )(place, raw_t, gains, seg_ids, x, g, b, c)


MIX_LANES = 512


def mix_kernel(
    x_ref, g_ref, b_ref, c_ref, seg_ref, skip_ref, cum2_ref, half_ref,
    y_ref, dx_ref, cpart_ref, ddt_ref, db_ref, dc_ref, dskip_ref,
    gram_ref, mask_ref, total_ref, cpart_sum_ref, ddt_sum_ref, dskip_sum_ref,
):
    step = pl.program_id(0)
    square = (BLOCK, BLOCK)

    @pl.when(step == 0)
    def _():
        seg_row = seg_ref[...]
        seg_col = jnp.broadcast_to(seg_row, square).T
        keep = (seg_row == seg_col) & (iota(square, 0) >= iota(square, 1))
        mask_ref[...] = jnp.where(keep, 0.0, -1e30)
        gram_ref[...] = dot_nt(c_ref[...], b_ref[...])
        total_ref[...] = jnp.zeros_like(total_ref)
        cpart_sum_ref[...] = jnp.zeros_like(cpart_sum_ref)
        ddt_sum_ref[...] = jnp.zeros_like(ddt_sum_ref)
        dskip_sum_ref[...] = jnp.zeros_like(dskip_sum_ref)

    lower = iota((BLOCK, 128), 1) < DIM
    zero = jnp.zeros((BLOCK, 128), BF16)
    cum2 = cum2_ref[...]
    columns = cum2.T
    for j in range(MIX_LANES // 128):
        head0 = step * (MIX_LANES // DIM) + 2 * j
        lanes = slice(j * 128, (j + 1) * 128)
        x_low = x_ref[:, lanes]
        g_low = g_ref[:, lanes]
        x = x_low.astype(F32)
        g = g_low.astype(F32)
        dt = dot(half_ref[2], spread(head0, 128))
        x_dt = (x * dt).astype(BF16)
        y = jnp.zeros((BLOCK, 128), F32)
        dx = jnp.zeros((BLOCK, 128), F32)
        for k in range(2):
            pick = lower if k == 0 else ~lower
            g_one = jnp.where(pick, g_low, zero)
            x_one = jnp.where(pick, x_dt, zero)
            head = 2 * j + k
            gap = columns[:, head : head + 1] - cum2[head : head + 1, :]
            kern = jnp.exp2(gap + mask_ref[...])
            mixed = (gram_ref[...] * kern).astype(BF16)
            total_ref[...] += dot_nt(g_one, x_dt) * kern
            y += dot(mixed, x_one)
            dx += dot_tn(mixed, g_one)
        skip = skip_ref[:, lanes]
        gather = gather_heads(head0, 256, 128)
        y_ref[:, lanes] = (y + skip * x).astype(BF16)
        dx_ref[:, lanes] = (dx * dt + skip * g).astype(BF16)
        apart = jnp.concatenate(split2(g * y - x_dt.astype(F32) * dx), axis=1)
        cpart_sum_ref[...] += dot(apart, gather)
        ddt_sum_ref[...] += dot((x * dx).astype(BF16), gather[:128])
        channel_sum = jnp.broadcast_to(jnp.sum(g * x, axis=0, keepdims=True), (8, 128))
        dskip_sum_ref[...] += dot(jnp.concatenate(split2(channel_sum), axis=1), gather)

    @pl.when(step == WIDTH // MIX_LANES - 1)
    def _():
        total = total_ref[...].astype(BF16)
        dc_ref[...] = dot(total, b_ref[...])
        db_ref[...] = dot_tn(total, c_ref[...])
        cpart_ref[...] = cpart_sum_ref[...].T
        ddt_ref[...] = ddt_sum_ref[...].T
        dskip_ref[...] = jnp.broadcast_to(dskip_sum_ref[:1], (128, HEADS)).T


def mix(x, g, b, c, seg, skip, cum2, half):
    return pl.pallas_call(
        mix_kernel,
        grid=(WIDTH // MIX_LANES,),
        in_specs=[
            wide(MIX_LANES), wide(MIX_LANES), whole(BLOCK, STATE), whole(BLOCK, STATE),
            whole(1, BLOCK),
            pl.BlockSpec((1, MIX_LANES), lambda i: (0, i)),
            pl.BlockSpec((MIX_LANES // DIM, BLOCK), lambda i: (i, 0)),
            whole(3, BLOCK, 2 * HEADS),
        ],
        out_specs=[
            wide(MIX_LANES), wide(MIX_LANES), whole(HEADS, BLOCK), whole(HEADS, BLOCK),
            whole(BLOCK, STATE), whole(BLOCK, STATE), whole(HEADS, 128),
        ],
        out_shape=[
            like((BLOCK, WIDTH), BF16), like((BLOCK, WIDTH), BF16),
            like((HEADS, BLOCK)), like((HEADS, BLOCK)),
            like((BLOCK, STATE)), like((BLOCK, STATE)), like((HEADS, 128)),
        ],
        scratch_shapes=[pltpu.VMEM((BLOCK, BLOCK), F32)] * 3
        + [pltpu.VMEM((BLOCK, HEADS), F32)] * 2
        + [pltpu.VMEM((8, HEADS), F32)],
        compiler_params=params(),
        cost_estimate=cost(20 * 10**9, 9 * 10**6, 4 * 10**6),
        name="mix",
    )(x, g, b, c, seg, skip, cum2, half)


def scan_kernel(pay_ref, out_ref, wide_ref, done_ref):
    wide_ref[...] = pay_ref[...].astype(F32)

    def row_of(k):
        return wide_ref[:, k, :]

    square = (PARTS, PARTS)
    high, mid, low, first, last = (row_of(CARRY + k) for k in range(5))
    upto = ones_where(iota(square, 0) >= iota(square, 1))
    through = dot(upto, high.astype(BF16)) + dot(upto, mid.astype(BF16)) + dot(upto, low.astype(BF16))
    ahead = through - (high + mid + low)
    through_t = through.T
    keep = (iota(square, 0) > iota(square, 1)) & (first[:, :1] == last.T[:1, :])
    forward, backward = [], []
    for lane in (0, DIM):
        gap = ahead[:, lane : lane + 1] - through_t[lane : lane + 1, :]
        carry = jnp.where(keep, jnp.exp(jnp.minimum(gap, 0.0)), 0.0)
        forward.append(carry.astype(BF16))
        backward.append(carry.T.astype(BF16))
    forward = jnp.concatenate(forward, axis=0)
    backward = jnp.concatenate(backward, axis=0)
    lower = iota((PARTS, 256), 1) & (128 - 1) < DIM

    for k in range(0, CARRY, 2):
        rows = jnp.concatenate([row_of(k), row_of(k + 1)], axis=1).astype(BF16)
        both = dot(forward if k < PIECE else backward, rows)
        pair = jnp.where(lower, both[:PARTS], both[PARTS:])
        done_ref[:, k, :] = pair[:, :128]
        done_ref[:, k + 1, :] = pair[:, 128:]
    out_ref[...] = done_ref[...].astype(BF16)


def scan(pay):
    return pl.pallas_call(
        scan_kernel,
        out_shape=like((PARTS, CARRY, 128), BF16),
        in_specs=[pl.BlockSpec(memory_space=pltpu.VMEM)],
        out_specs=pl.BlockSpec(memory_space=pltpu.VMEM),
        scratch_shapes=[
            pltpu.VMEM((PARTS, CARRY + META, 128), F32),
            pltpu.VMEM((PARTS, CARRY, 128), F32),
        ],
        compiler_params=params(),
        cost_estimate=cost(5 * 10**8, 5 * 10**6, 10**5),
        name="scan",
    )(pay)


def carried(state_ref, j):
    tiles = [state_ref[k * ROWS : (k + 1) * ROWS] for k in (2 * j, 2 * j + 1)]
    h_low = jnp.concatenate([tile[:, :PIECE].reshape(STATE, 128) for tile in tiles], axis=1)
    lam_low = jnp.concatenate([tile[:, PIECE:].reshape(STATE, 128) for tile in tiles], axis=1)
    return h_low, lam_low


SUMS_LANES = 1024


def sums_kernel(
    x_ref, g_ref, state_ref, b_ref, c_ref, scal_ref, raw_ref, rate_ref,
    cpart_ref, ddt_ref, dskip_ref,
    raw_grad_ref, sums_ref,
    dstart_ref, dweight_ref, ddecay_ref,
):
    step = pl.program_id(0)

    @pl.when(step == 0)
    def _():
        dstart_ref[...] = jnp.zeros_like(dstart_ref)
        dweight_ref[...] = jnp.zeros_like(dweight_ref)
        ddecay_ref[...] = jnp.zeros_like(ddecay_ref)

    for j in range(SUMS_LANES // 256):
        lanes = slice(j * 256, (j + 1) * 256)
        gather = gather_heads(step * (SUMS_LANES // DIM) + 4 * j, 256, 256)
        h_low, lam_low = carried(state_ref, j)
        from_state = dot(c_ref[...], h_low)
        from_grad = dot(b_ref[...], lam_low)
        dstart_ref[...] += dot((g_ref[:, lanes].astype(F32) * from_state).astype(BF16), gather)
        dweight_ref[...] += dot((x_ref[:, lanes].astype(F32) * from_grad).astype(BF16), gather)
        ddecay_ref[...] += dot((h_low.astype(F32) * lam_low.astype(F32)).astype(BF16), gather)

    @pl.when(step == WIDTH // SUMS_LANES - 1)
    def _():
        end, weight, start, dt = (scal_ref[k] for k in range(4))
        d_weight = dweight_ref[...].T
        used = d_weight * weight
        d_cum = cpart_ref[...] + dstart_ref[...].T * start - used
        at_last = iota((HEADS, BLOCK), 1) == BLOCK - 1
        d_decay = jnp.sum(ddecay_ref[...].T, axis=1, keepdims=True)
        d_total = jnp.sum(used, axis=1, keepdims=True) + d_decay * start[:, BLOCK - 1 :]
        d_cum = d_cum + jnp.where(at_last, d_total, 0.0)
        square = (BLOCK, BLOCK)
        onward = ones_where(iota(square, 0) >= iota(square, 1))
        high, mid, low = split3(d_cum)
        d_log = dot(high, onward) + dot(mid, onward) + dot(low, onward)
        rate = rate_ref[:, :1]
        d_dt = ddt_ref[...] + d_weight * end - rate * d_log
        raw = raw_ref[...].astype(F32)
        raw_grad_ref[...] = (d_dt / (1.0 + jnp.exp(-raw))).astype(BF16)
        rate_grad = -jnp.sum(dt * d_log, axis=1, keepdims=True) * rate
        column = jnp.concatenate([rate_grad, dskip_ref[:, :1]], axis=0)
        sums_ref[...] = jnp.broadcast_to(column, (PARTS, 128)).T


def gradient_sums(x, g, state, b, c, scal, raw_t, rate, cpart, ddt, dskip):
    return pl.pallas_call(
        sums_kernel,
        grid=(WIDTH // SUMS_LANES,),
        in_specs=[
            wide(SUMS_LANES), wide(SUMS_LANES), pieces(SUMS_LANES, CARRY),
            whole(BLOCK, STATE), whole(BLOCK, STATE),
            whole(4, HEADS, BLOCK), whole(HEADS, BLOCK), whole(HEADS, 128),
            whole(HEADS, BLOCK), whole(HEADS, BLOCK), whole(HEADS, 128),
        ],
        out_specs=[whole(HEADS, BLOCK), whole(PARTS, 128)],
        out_shape=[like((HEADS, BLOCK), BF16), like((PARTS, 128))],
        scratch_shapes=[
            pltpu.VMEM((BLOCK, HEADS), F32),
            pltpu.VMEM((BLOCK, HEADS), F32),
            pltpu.VMEM((STATE, HEADS), F32),
        ],
        compiler_params=params(),
        cost_estimate=cost(10**9, 8 * 10**6, 10**5),
        name="gradient_sums",
    )(x, g, state, b, c, scal, raw_t, rate, cpart, ddt, dskip)


FINISH_LANES = 512


def finish_kernel(
    x_ref, g_ref, ymix_ref, dxmix_ref, state_ref, b_ref, c_ref, half_ref, dbmix_ref, dcmix_ref,
    y_ref, dx_ref, db_ref, dc_ref,
):
    step = pl.program_id(0)

    @pl.when(step == 0)
    def _():
        db_ref[...] = dbmix_ref[...]
        dc_ref[...] = dcmix_ref[...]

    for j in range(FINISH_LANES // 256):
        copy = spread(step * (FINISH_LANES // DIM) + 4 * j, 256)
        lanes = slice(j * 256, (j + 1) * 256)
        x = x_ref[:, lanes].astype(F32)
        g = g_ref[:, lanes].astype(F32)
        h_low, lam_low = carried(state_ref, j)
        weight = dot(half_ref[0], copy)
        start = dot(half_ref[1], copy)
        from_state = dot(c_ref[...], h_low)
        from_grad = dot(b_ref[...], lam_low)
        y_ref[:, lanes] = (ymix_ref[:, lanes].astype(F32) + start * from_state).astype(BF16)
        dx_ref[:, lanes] = (dxmix_ref[:, lanes].astype(F32) + weight * from_grad).astype(BF16)
        dc_ref[...] += dot_nt((start * g).astype(BF16), h_low)
        db_ref[...] += dot_nt((weight * x).astype(BF16), lam_low)


def finish(x, g, ymix, dxmix, state, b, c, half, dbmix, dcmix):
    lanes = FINISH_LANES
    return pl.pallas_call(
        finish_kernel,
        grid=(WIDTH // lanes,),
        in_specs=[
            wide(lanes), wide(lanes), wide(lanes), wide(lanes), pieces(lanes, CARRY),
            whole(BLOCK, STATE), whole(BLOCK, STATE),
            whole(3, BLOCK, 2 * HEADS), whole(BLOCK, STATE), whole(BLOCK, STATE),
        ],
        out_specs=[wide(lanes), wide(lanes), whole(BLOCK, STATE), whole(BLOCK, STATE)],
        out_shape=[
            like((BLOCK, WIDTH), BF16), like((BLOCK, WIDTH), BF16),
            like((BLOCK, STATE)), like((BLOCK, STATE)),
        ],
        compiler_params=params(),
        cost_estimate=cost(8 * 10**9, 16 * 10**6, 10**5),
        name="finish",
    )(x, g, ymix, dxmix, state, b, c, half, dbmix, dcmix)


def body(inputs, dt_raw, b_proj, c_proj, a_log, d_skip, seg_ids, cotangent):
    everyone = ("seq", "head")
    mine = lax.axis_index("head")
    place = mine.astype(jnp.int32).reshape(1)
    group = a_log.shape[0]
    gains = lax.all_gather(jnp.stack([a_log, d_skip]), "head", tiled=True)
    skip = jnp.broadcast_to(gains[1::2].reshape(HEADS, 1), (HEADS, DIM)).reshape(1, WIDTH)
    raw_t = dt_raw.T
    pay, scal, cum2, half, rate, seg = states(
        place, raw_t, gains, seg_ids.reshape(-1, 128), inputs, cotangent, b_proj, c_proj
    )
    pay = lax.all_to_all(pay, everyone, 0, 0, tiled=True)
    ymix, dxmix, cpart, ddt, dbmix, dcmix, dskip = mix(
        inputs, cotangent, b_proj, c_proj, seg, skip, cum2, half
    )
    state = lax.all_to_all(scan(pay), everyone, 0, 0, tiled=True)
    raw_grad, sums = gradient_sums(
        inputs, cotangent, state, b_proj, c_proj, scal, raw_t, rate, cpart, ddt, dskip
    )
    sums = lax.all_to_all(sums.reshape(PARTS, 1, 128), everyone, 0, 0, tiled=True)
    y, dx, db, dc = finish(
        inputs, cotangent, ymix, dxmix, state, b_proj, c_proj, half, dbmix, dcmix
    )
    sums = jnp.sum(sums, axis=(0, 1))
    a_grad = lax.dynamic_slice(sums, (mine * group,), (group,))
    skip_grad = lax.dynamic_slice(sums, (HEADS + mine * group,), (group,))
    return (y, dx, raw_grad.T, db, dc, a_grad, skip_grad)


def solution(mesh):
    tokens = P(("seq", "head"), None)
    in_specs = (tokens, tokens, tokens, tokens, P("head"), P("head"), P("seq"), tokens)
    out_specs = (tokens, tokens, tokens, tokens, tokens, P("head"), P("head"))
    return jax.shard_map(body, mesh=mesh, in_specs=in_specs, out_specs=out_specs, check_vma=False)
```

profile of v0, /device:TPU:1, one launch (start us, length us, event | category | flops | bytes accessed | tf_op | source)
XLA Modules:
  0.0 134.0 jit_solution(7480244456583227022)
XLA Ops:
  0.6 0.7 maximum_bitcast_fusion
  1.3 8.8 %all-gather = f32[4,2,16]{2,1,0:T(2,128)S(1)} all-gather(f32[1,2,16]{2,1,0:T(2,128)S(1)} %maximum_bitcast_fusion), channel_id=1, replica_groups=mesh['head'=4,'seq'=32] {'head'}, dimensions={0}, use_global_device_ids=true | all-gather | bytes 640 | tf_op jit(solution)/shard_map/all_gather | solution.py:463
  10.1 1.6 %copy-done = bf16[256,4096]{1,0:T(8,128)(2,1)S(1)} copy-done((bf16[256,4096]{1,0:T(8,128)(2,1)S(1)}, bf16[256,4096]{1,0:T(8,128)(2,1)}, u32[]{:S(2)}) %copy-start) | copy-done | bytes 2097176
  11.7 1.6 %copy-done.2 = bf16[256,4096]{1,0:T(8,128)(2,1)S(1)} copy-done((bf16[256,4096]{1,0:T(8,128)(2,1)S(1)}, bf16[256,4096]{1,0:T(8,128)(2,1)}, u32[]{:S(2)}) %copy-start.2) | copy-done | bytes 2097176
  13.3 0.8 copy-done.7
  14.1 0.8 copy-done.9
  15.0 0.8 copy-done.11
  15.7 0.7 copy-done.13
  16.4 4.1 %states.1 = (bf16[128,72,128]{2,1,0:T(8,128)(2,1)S(1)}, f32[4,64,256]{2,1,0:T(8,128)S(1)}, f32[64,256]{1,0:T(8,128)S(1)}, bf16[3,256,128]{2,1,0:T(8,128)(2,1)S(1...) custom-call(s32[1]{0:T(128)} %bitcast.place_ref, bf16[64,256]{1,0:T(8,128)(2,1)S(1)} %bitcast.12, f32[8,16]{1,0:T(8,128)S(1)} %bitcast.14, ...), custom_call_target="tpu_custom_call" | custom-call | flops 1000000000 | bytes 8000000 | tf_op jit(solution)/shard_map/states/pallas_call | solution.py:154
  20.6 43.5 %all_to_all.15.pay_ref = bf16[128,72,128]{2,1,0:T(8,128)(2,1)S(1)} all-to-all(bf16[128,72,128]{2,1,0:T(8,128)(2,1)S(1)} %get-tuple-element.31), channel_id=1, replica_groups=mesh['head'=4,'seq'=32] {'seq','head'}, dimensions={0} | all-to-all | bytes 4718592 | tf_op jit(solution)/shard_map/all_to_all | solution.py:469
  64.1 6.6 %scan.1 = bf16[128,64,128]{2,1,0:T(8,128)(2,1)S(1)} custom-call(bf16[128,72,128]{2,1,0:T(8,128)(2,1)S(1)} %all_to_all.15.pay_ref), custom_call_target="tpu_custom_call" | custom-call | flops 500000000 | bytes 5000000 | tf_op jit(solution)/shard_map/scan/pallas_call | solution.py:312
  70.7 1.3 copy-done.6
  72.0 5.0 %all-to-all-start.1 = ((bf16[128,64,128]{2,1,0:T(8,128)(2,1)}), bf16[128,64,128]{2,1,0:T(8,128)(2,1)}, u32[]{:S(2)}, u32[]{:S(2)}) async-start(bf16[128,64,128]{2,1,0:T(8,128)(2,1)} %copy-done.6), calls=%async_computation.1 | async-start | bytes 4194304 | tf_op jit(solution)/shard_map/all_to_all | solution.py:473
  77.0 0.1 broadcast_in_dim.7
  77.1 0.1 broadcast_in_dim.8
  77.2 0.1 reshape.30.skip_ref
  77.3 0.0 copy-start.3
  77.3 1.6 %copy-done.3 = bf16[256,4096]{1,0:T(8,128)(2,1)S(1)} copy-done((bf16[256,4096]{1,0:T(8,128)(2,1)S(1)}, bf16[256,4096]{1,0:T(8,128)(2,1)}, u32[]{:S(2)}) %copy-start.3) | copy-done | bytes 2097176
  78.9 20.6 %mix.1 = (bf16[256,4096]{1,0:T(8,128)(2,1)S(1)}, bf16[256,4096]{1,0:T(8,128)(2,1)S(1)}, f32[64,256]{1,0:T(8,128)S(1)}, f32[64,256]{1,0:T(8,128)S(1)}, f32[256,12...) custom-call(bf16[256,4096]{1,0:T(8,128)(2,1)S(1)} %copy-done.1, bf16[256,4096]{1,0:T(8,128)(2,1)S(1)} %copy-done.3, ...), custom_call_target="tpu_custom_call" | custom-call | flops 20000000000 | bytes 9000000 | tf_op jit(solution)/shard_map/mix/pallas_call | solution.py:251
  99.5 0.0 copy-start.14
  99.5 1.3 copy-done.14
  100.8 1.3 copy-done.16
  102.1 5.1 %all-to-all-done.1.state_ref = bf16[128,64,128]{2,1,0:T(8,128)(2,1)} async-done(((bf16[128,64,128]{2,1,0:T(8,128)(2,1)}), bf16[128,64,128]{2,1,0:T(8,128)(2,1)}, u32[]{:S(2)}, u32[]{:S(2)}) %all-to-all-start.1) | async-done | bytes 2097184 | tf_op jit(solution)/shard_map/all_to_all | solution.py:473
  107.3 1.6 %copy-done.4 = bf16[256,4096]{1,0:T(8,128)(2,1)S(1)} copy-done((bf16[256,4096]{1,0:T(8,128)(2,1)S(1)}, bf16[256,4096]{1,0:T(8,128)(2,1)}, u32[]{:S(2)}) %copy-start.4) | copy-done | bytes 2097176
  108.9 6.9 %gradient_sums.1 = (bf16[64,256]{1,0:T(8,128)(2,1)}, f32[128,128]{1,0:T(8,128)}) custom-call(bf16[256,4096]{1,0:T(8,128)(2,1)S(1)} %copy-done.1, bf16[256,4096]{1,0:T(8,128)(2,1)S(1)} %copy-done.4, bf16[128,64,128]{2,1,0:T(8,128)(2,1)} %all-to-all-done.1.state_ref, bf16[256,128]{1,0:T(8,128)(2,1)S(1)} %copy-done.8, bf16[256,128]{1,0:T(8,128)(2,1)S(1)} %copy-done.10, ...), custom_call_target="tpu_custom_call" | custom-call | flops 1000000000 | bytes 8000000 | tf_op jit(solution)/shard_map/gradient_sums/pallas_call | solution.py:385
  115.7 4.7 %all-to-all-start.2 = ((f32[128,1,128]{2,1,0:T(1,128)}), f32[128,1,128]{2,1,0:T(1,128)S(1)}, u32[]{:S(2)}, u32[]{:S(2)}) async-start(f32[128,1,128]{2,1,0:T(1,128)} %bitcast.9), calls=%async_computation.2 | async-start | bytes 131072 | tf_op jit(solution)/shard_map/all_to_all | solution.py:477
  120.4 1.6 %copy-done.5 = bf16[256,4096]{1,0:T(8,128)(2,1)S(1)} copy-done((bf16[256,4096]{1,0:T(8,128)(2,1)S(1)}, bf16[256,4096]{1,0:T(8,128)(2,1)}, u32[]{:S(2)}) %copy-start.5) | copy-done | bytes 2097176
  122.0 1.6 %copy-done.15 = bf16[256,4096]{1,0:T(8,128)(2,1)S(1)} copy-done((bf16[256,4096]{1,0:T(8,128)(2,1)S(1)}, bf16[256,4096]{1,0:T(8,128)(2,1)}, u32[]{:S(2)}) %copy-start.15) | copy-done | bytes 2097176
  123.6 1.6 %copy-done.17 = bf16[256,4096]{1,0:T(8,128)(2,1)S(1)} copy-done((bf16[256,4096]{1,0:T(8,128)(2,1)S(1)}, bf16[256,4096]{1,0:T(8,128)(2,1)}, u32[]{:S(2)}) %copy-start.17) | copy-done | bytes 2097176
  125.2 8.1 %finish.1 = (bf16[256,4096]{1,0:T(8,128)(2,1)}, bf16[256,4096]{1,0:T(8,128)(2,1)}, f32[256,128]{1,0:T(8,128)}, f32[256,128]{1,0:T(8,128)}) custom-call(bf16[256,4096]{1,0:T(8,128)(2,1)S(1)} %copy-done.1, bf16[256,4096]{1,0:T(8,128)(2,1)S(1)} %copy-done.5, bf16[256,4096]{1,0:T(8,128)(2,1)S(1)} %copy-done.15, bf16[256,4096]{1,0:T(8,128)(2,1)S(1)} %copy-done.17, ...), custom_call_target="tpu_custom_call" | custom-call | flops 8000000000 | bytes 16000000 | tf_op jit(solution)/shard_map/finish/pallas_call | solution.py:439
  133.3 0.2 reduce_sum.9
  133.4 0.6 fusion
  (22 shorter events, 0.1 us)
Async XLA Ops:
  10.1 1.6 %copy-start = (bf16[256,4096]{1,0:T(8,128)(2,1)S(1)}, bf16[256,4096]{1,0:T(8,128)(2,1)}, u32[]{:S(2)}) copy-start(bf16[256,4096]{1,0:T(8,128)(2,1)} %x_ref.7) | copy-start | bytes 6291460
  11.7 1.6 %copy-start.2 = (bf16[256,4096]{1,0:T(8,128)(2,1)S(1)}, bf16[256,4096]{1,0:T(8,128)(2,1)}, u32[]{:S(2)}) copy-start(bf16[256,4096]{1,0:T(8,128)(2,1)} %g_ref.7) | copy-start | bytes 6291460
  13.3 0.8 copy-start.7
  14.1 0.8 copy-start.9
  15.0 0.8 copy-start.11
  15.7 0.7 copy-start.13
  70.7 1.3 copy-start.6
  72.0 5.3 %copy-start.1 = (bf16[256,4096]{1,0:T(8,128)(2,1)S(1)}, bf16[256,4096]{1,0:T(8,128)(2,1)}, u32[]{:S(2)}) copy-start(bf16[256,4096]{1,0:T(8,128)(2,1)} %x_ref.7) | copy-start | bytes 6291460
  72.0 5.3 %copy-start.8 = (bf16[256,128]{1,0:T(8,128)(2,1)S(1)}, bf16[256,128]{1,0:T(8,128)(2,1)}, u32[]{:S(2)}) copy-start(bf16[256,128]{1,0:T(8,128)(2,1)} %b_ref.7) | copy-start | bytes 196612
  72.0 5.3 %copy-start.10 = (bf16[256,128]{1,0:T(8,128)(2,1)S(1)}, bf16[256,128]{1,0:T(8,128)(2,1)}, u32[]{:S(2)}) copy-start(bf16[256,128]{1,0:T(8,128)(2,1)} %c_ref.7) | copy-start | bytes 196612
  72.0 35.3 %all-to-all-start.1 = ((bf16[128,64,128]{2,1,0:T(8,128)(2,1)}), bf16[128,64,128]{2,1,0:T(8,128)(2,1)}, u32[]{:S(2)}, u32[]{:S(2)}) async-start(bf16[128,64,128]{2,1,0:T(8,128)(2,1)} %copy-done.6), calls=%async_computation.1 | async-start | bytes 4194304 | tf_op jit(solution)/shard_map/all_to_all | solution.py:473
  77.3 1.6 %copy-start.3 = (bf16[256,4096]{1,0:T(8,128)(2,1)S(1)}, bf16[256,4096]{1,0:T(8,128)(2,1)}, u32[]{:S(2)}) copy-start(bf16[256,4096]{1,0:T(8,128)(2,1)} %g_ref.7) | copy-start | bytes 6291460
  78.9 28.3 %copy-start.12 = (bf16[256,64]{0,1:T(8,128)(2,1)S(1)}, bf16[256,64]{0,1:T(8,128)(2,1)}, u32[]{:S(2)}) copy-start(bf16[256,64]{0,1:T(8,128)(2,1)} %param.9) | copy-start | bytes 98308
  99.5 1.3 copy-start.14
  100.8 1.3 copy-start.16
  107.3 1.6 %copy-start.4 = (bf16[256,4096]{1,0:T(8,128)(2,1)S(1)}, bf16[256,4096]{1,0:T(8,128)(2,1)}, u32[]{:S(2)}) copy-start(bf16[256,4096]{1,0:T(8,128)(2,1)} %g_ref.7) | copy-start | bytes 6291460
  115.7 17.6 %all-to-all-start.2 = ((f32[128,1,128]{2,1,0:T(1,128)}), f32[128,1,128]{2,1,0:T(1,128)S(1)}, u32[]{:S(2)}, u32[]{:S(2)}) async-start(f32[128,1,128]{2,1,0:T(1,128)} %bitcast.9), calls=%async_computation.2 | async-start | bytes 131072 | tf_op jit(solution)/shard_map/all_to_all | solution.py:477
  120.4 1.6 %copy-start.5 = (bf16[256,4096]{1,0:T(8,128)(2,1)S(1)}, bf16[256,4096]{1,0:T(8,128)(2,1)}, u32[]{:S(2)}) copy-start(bf16[256,4096]{1,0:T(8,128)(2,1)} %g_ref.7) | copy-start | bytes 6291460
  122.0 1.6 %copy-start.15 = (bf16[256,4096]{1,0:T(8,128)(2,1)S(1)}, bf16[256,4096]{1,0:T(8,128)(2,1)}, u32[]{:S(2)}) copy-start(bf16[256,4096]{1,0:T(8,128)(2,1)} %copy-done.14) | copy-start | bytes 6291460
  123.6 1.6 %copy-start.17 = (bf16[256,4096]{1,0:T(8,128)(2,1)S(1)}, bf16[256,4096]{1,0:T(8,128)(2,1)}, u32[]{:S(2)}) copy-start(bf16[256,4096]{1,0:T(8,128)(2,1)} %copy-done.16) | copy-start | bytes 6291460
where the time goes:
time: 135 us; the launch traced here: 134 us
  blocking collectives  52.3 us (39%)
  Pallas kernels  46.2 us (34%)
  local copies, waits for them, and re-layouts  19.1 us (14%)
  starting transfers between devices  9.72 us (7%)
  waiting for transfers between devices  5.12 us (4%)
    all_to_all x1, blocking collectives, body(): pay = lax.all_to_all(pay, everyone, 0, 0, tiled=True)  43.5 us
    pallas_call x1, Pallas kernels, mix(): pl.pallas_call(mix_kernel, grid=(WIDTH // MIX_LANES,), in_specs=[wide(MIX...  20.6 us
    unnamed x36, local copies, waits for them, and re-layouts  18.2 us
    all_gather x1, blocking collectives, body(): gains = lax.all_gather(jnp.stack([a_log, d_skip]), 'head', tiled=True)  8.78 us
    pallas_call x1, Pallas kernels, finish(): pl.pallas_call(finish_kernel, grid=(WIDTH // lanes,), in_specs=[wide(lane...  8.08 us
    pallas_call x1, Pallas kernels, gradient_sums(): pl.pallas_call(sums_kernel, grid=(WIDTH // SUMS_LANES,), in_specs=[wide(S...  6.86 us
    pallas_call x1, Pallas kernels, scan(): pl.pallas_call(scan_kernel, out_shape=like((PARTS, CARRY, 128), BF16), in...  6.58 us
    all_to_all x1, waiting for transfers between devices, body(): state = lax.all_to_all(scan(pay), everyone, 0, 0, tiled=True)  5.12 us
  transfers between devices with their start and end apart: 2, of which 1 were waited for; matrix products, arithmetic and copies ran while one was open for 0% of the time, Pallas kernels for 21%

commit v1 on v0

--- a/solution.py
+++ b/solution.py
@@ -72,7 +72,7 @@
     return pl.BlockSpec((PARTS * lanes // WIDTH, rows, 128), lambda i: (i, 0, 0))
 
 
-def params(mib=24):
+def params(mib=60):
     return pltpu.CompilerParams(vmem_limit_bytes=mib * 1024 * 1024)
 
 
@@ -84,7 +84,7 @@
     return jax.ShapeDtypeStruct(shape, kind)
 
 
-STATES_LANES = 1024
+STATES_LANES = 2048
 
 
 def states_kernel(
@@ -276,14 +276,10 @@
     )(x, g, b, c, seg, skip, cum2, half)
 
 
-def scan_kernel(pay_ref, out_ref, wide_ref, done_ref):
-    wide_ref[...] = pay_ref[...].astype(F32)
-
-    def row_of(k):
-        return wide_ref[:, k, :]
-
+def scan_kernel(pay_ref, out_ref):
     square = (PARTS, PARTS)
-    high, mid, low, first, last = (row_of(CARRY + k) for k in range(5))
+    notes = jnp.swapaxes(pay_ref[:, CARRY:, :].astype(F32), 0, 1)
+    high, mid, low, first, last = (notes[k] for k in range(5))
     upto = ones_where(iota(square, 0) >= iota(square, 1))
     through = dot(upto, high.astype(BF16)) + dot(upto, mid.astype(BF16)) + dot(upto, low.astype(BF16))
     ahead = through - (high + mid + low)
@@ -299,13 +295,15 @@
     backward = jnp.concatenate(backward, axis=0)
     lower = iota((PARTS, 256), 1) & (128 - 1) < DIM
 
-    for k in range(0, CARRY, 2):
-        rows = jnp.concatenate([row_of(k), row_of(k + 1)], axis=1).astype(BF16)
-        both = dot(forward if k < PIECE else backward, rows)
-        pair = jnp.where(lower, both[:PARTS], both[PARTS:])
-        done_ref[:, k, :] = pair[:, :128]
-        done_ref[:, k + 1, :] = pair[:, 128:]
-    out_ref[...] = done_ref[...].astype(BF16)
+    for k in range(0, CARRY, 16):
+        block = jnp.swapaxes(pay_ref[:, k : k + 16, :], 0, 1)
+        done = []
+        for i in range(0, 16, 2):
+            rows = jnp.concatenate([block[i], block[i + 1]], axis=1)
+            both = dot(forward if k < PIECE else backward, rows)
+            pair = jnp.where(lower, both[:PARTS], both[PARTS:]).astype(BF16)
+            done += [pair[:, :128], pair[:, 128:]]
+        out_ref[:, k : k + 16, :] = jnp.swapaxes(jnp.stack(done), 0, 1)
 
 
 def scan(pay):
@@ -314,11 +312,7 @@
         out_shape=like((PARTS, CARRY, 128), BF16),
         in_specs=[pl.BlockSpec(memory_space=pltpu.VMEM)],
         out_specs=pl.BlockSpec(memory_space=pltpu.VMEM),
-        scratch_shapes=[
-            pltpu.VMEM((PARTS, CARRY + META, 128), F32),
-            pltpu.VMEM((PARTS, CARRY, 128), F32),
-        ],
-        compiler_params=params(),
+        compiler_params=params(16),
         cost_estimate=cost(5 * 10**8, 5 * 10**6, 10**5),
         name="scan",
     )(pay)
@@ -331,7 +325,7 @@
     return h_low, lam_low
 
 
-SUMS_LANES = 1024
+SUMS_LANES = 2048
 
 
 def sums_kernel(
@@ -404,7 +398,7 @@
     )(x, g, state, b, c, scal, raw_t, rate, cpart, ddt, dskip)
 
 
-FINISH_LANES = 512
+FINISH_LANES = 1024
 
 
 def finish_kernel(

time: 135 us -> 121 us (0.90)
  local copies, waits for them, and re-layouts: 19.1 us -> 2.79 us
  waiting for transfers between devices: 5.12 us -> 8.47 us
  starting transfers between devices: 9.72 us -> 7.69 us
    unnamed x36 -> x4, local copies, waits for them, and re-layouts: 18.2 us -> 1.33 us
    pallas_call x1, Pallas kernels: 6.58 us -> 3.58 us  [scan(): pl.pallas_call(scan_kernel, out_shape=like((PARTS, CARRY, 128), BF16), in...]
    all_to_all x1, waiting for transfers between devices: 5.12 us -> 7.38 us  [body(): state = lax.all_to_all(scan(pay), everyone, 0, 0, tiled=True)]
    pallas_call x1, Pallas kernels: 20.6 us -> 22.4 us  [mix(): pl.pallas_call(mix_kernel, grid=(WIDTH // MIX_LANES,), in_specs=[wide(MIX...]
  transfers between devices with their start and end apart: 2 -> 2, of which waited for: 1 -> 2; matrix products, arithmetic and copies ran while one was open for 0% -> 1% of each run, Pallas kernels for 21% -> 26%
where the time goes in v1:
time: 121 us
  blocking collectives  52.9 us (44%)
  Pallas kernels  47.5 us (39%)
  waiting for transfers between devices  8.47 us (7%)
  starting transfers between devices  7.69 us (6%)
  local copies, waits for them, and re-layouts  2.79 us (2%)
    all_to_all x1, blocking collectives, body(): pay = lax.all_to_all(pay, everyone, 0, 0, tiled=True)  43.7 us
    pallas_call x1, Pallas kernels, mix(): pl.pallas_call(mix_kernel, grid=(WIDTH // MIX_LANES,), in_specs=[wide(MIX...  22.4 us
    all_gather x1, blocking collectives, body(): gains = lax.all_gather(jnp.stack([a_log, d_skip]), 'head', tiled=True)  9.2 us
    pallas_call x1, Pallas kernels, finish(): pl.pallas_call(finish_kernel, grid=(WIDTH // lanes,), in_specs=[wide(lane...  8.55 us
    pallas_call x1, Pallas kernels, gradient_sums(): pl.pallas_call(sums_kernel, grid=(WIDTH // SUMS_LANES,), in_specs=[wide(S...  7.68 us
    all_to_all x1, waiting for transfers between devices, body(): state = lax.all_to_all(scan(pay), everyone, 0, 0, tiled=True)  7.38 us
    pallas_call x1, Pallas kernels, states(): pl.pallas_call(states_kernel, grid=(WIDTH // STATES_LANES,), in_specs=[pl...  5.31 us
    all_to_all x1, starting transfers between devices, body(): state = lax.all_to_all(scan(pay), everyone, 0, 0, tiled=True)  3.88 us
  transfers between devices with their start and end apart: 2, of which 2 were waited for; matrix products, arithmetic and copies ran while one was open for 1% of the time, Pallas kernels for 26%

profile of v1, /device:TPU:1, one launch (start us, length us, event | category | flops | bytes accessed | tf_op | source)
XLA Modules:
  0.0 120.9 jit_solution(11536597382534422052)
XLA Ops:
  0.6 0.7 maximum_bitcast_fusion
  1.3 9.2 %all-gather = f32[4,2,16]{2,1,0:T(2,128)} all-gather(f32[1,2,16]{2,1,0:T(2,128)S(1)} %maximum_bitcast_fusion), channel_id=1, replica_groups=mesh['head'=4,'seq'=32] {'head'}, dimensions={0}, use_global_device_ids=true | all-gather | bytes 640 | tf_op jit(solution)/shard_map/all_gather | solution.py:457
  10.5 5.3 %states.1 = (bf16[128,72,128]{2,1,0:T(8,128)(2,1)}, f32[4,64,256]{2,1,0:T(8,128)}, f32[64,256]{1,0:T(8,128)}, bf16[3,256,128]{2,1,0:T(8,128)(2,1)}, f32[64,128]{1,0:T(8,128)}, /*index=5*/f32[1,256]{1,0:T(1,128)}) custom-call(s32[1]{0:T(128)} %bitcast.place_ref, bf16[64,256]{1,0:T(8,128)(2,1)} %bitcast.12, f32[8,16]{1,0:T(8,128)} %bitcast.15, ...), custom_call_target="tpu_custom_call" | custom-call | flops 1000000000 | bytes 8000000 | tf_op jit(solution)/shard_map/states/pallas_call | solution.py:154
  15.8 43.7 %all_to_all.15.pay_ref = bf16[128,72,128]{2,1,0:T(8,128)(2,1)S(1)} all-to-all(bf16[128,72,128]{2,1,0:T(8,128)(2,1)} %get-tuple-element.31), channel_id=1, replica_groups=mesh['head'=4,'seq'=32] {'seq','head'}, dimensions={0} | all-to-all | bytes 4718592 | tf_op jit(solution)/shard_map/all_to_all | solution.py:463
  59.5 3.6 %scan.1 = bf16[128,64,128]{2,1,0:T(8,128)(2,1)} custom-call(bf16[128,72,128]{2,1,0:T(8,128)(2,1)S(1)} %all_to_all.15.pay_ref), custom_call_target="tpu_custom_call" | custom-call | flops 500000000 | bytes 5000000 | tf_op jit(solution)/shard_map/scan/pallas_call | solution.py:310
  63.1 0.0 copy-start.1
  63.1 3.9 %all-to-all-start.1 = ((bf16[128,64,128]{2,1,0:T(8,128)(2,1)}), bf16[128,64,128]{2,1,0:T(8,128)(2,1)S(1)}, u32[]{:S(2)}, u32[]{:S(2)}) async-start(bf16[128,64,128]{2,1,0:T(8,128)(2,1)} %scan.1), calls=%async_computation.1 | async-start | bytes 4194304 | tf_op jit(solution)/shard_map/all_to_all | solution.py:467
  67.0 0.0 copy-done.1
  67.0 0.1 broadcast_in_dim.7
  67.1 0.1 broadcast_in_dim.8
  67.2 0.7 reshape.30.skip_ref
  67.9 22.4 %mix.1 = (bf16[256,4096]{1,0:T(8,128)(2,1)}, bf16[256,4096]{1,0:T(8,128)(2,1)}, f32[64,256]{1,0:T(8,128)}, f32[64,256]{1,0:T(8,128)}, f32[256,128]{1,0:T(8,128)}, /*index=5*/f32[256,128]{1,0:T(8,128)}, f32[64,128]{1,0:T(8,128)}) custom-call(bf16[256,4096]{1,0:T(8,128)(2,1)} %x_ref.7, bf16[256,4096]{1,0:T(8,128)(2,1)} %g_ref.7, bf16[256,128]{1,0:T(8,128)(2,1)} %b_ref.7, ...), custom_call_target="tpu_custom_call" | custom-call | flops 20000000000 | bytes 9000000 | tf_op jit(solution)/shard_map/mix/pallas_call | solution.py:251
  90.3 7.4 %all-to-all-done.1.state_ref = bf16[128,64,128]{2,1,0:T(8,128)(2,1)S(1)} async-done(((bf16[128,64,128]{2,1,0:T(8,128)(2,1)}), bf16[128,64,128]{2,1,0:T(8,128)(2,1)S(1)}, u32[]{:S(2)}, u32[]{:S(2)}) %all-to-all-start.1) | async-done | bytes 2097184 | tf_op jit(solution)/shard_map/all_to_all | solution.py:467
  97.7 0.0 copy-start
  97.7 1.3 %copy-done = bf16[128,64,128]{2,1,0:T(8,128)(2,1)} copy-done((bf16[128,64,128]{2,1,0:T(8,128)(2,1)}, bf16[128,64,128]{2,1,0:T(8,128)(2,1)S(1)}, u32[]{:S(2)}) %copy-start) | copy-done | bytes 2097176
  99.0 7.7 %gradient_sums.1 = (bf16[64,256]{1,0:T(8,128)(2,1)}, f32[128,128]{1,0:T(8,128)}) custom-call(bf16[256,4096]{1,0:T(8,128)(2,1)} %x_ref.7, bf16[256,4096]{1,0:T(8,128)(2,1)} %g_ref.7, bf16[128,64,128]{2,1,0:T(8,128)(2,1)} %copy-done, bf16[256,128]{1,0:T(8,128)(2,1)} %b_ref.7, bf16[256,128]{1,0:T(8,128)(2,1)} %c_ref.7, ...), custom_call_target="tpu_custom_call" | custom-call | flops 1000000000 | bytes 8000000 | tf_op jit(solution)/shard_map/gradient_sums/pallas_call | solution.py:379
  106.7 3.8 %all-to-all-start.2 = ((f32[128,1,128]{2,1,0:T(1,128)}), f32[128,1,128]{2,1,0:T(1,128)S(1)}, u32[]{:S(2)}, u32[]{:S(2)}) async-start(f32[128,1,128]{2,1,0:T(1,128)} %bitcast.14), calls=%async_computation.2 | async-start | bytes 131072 | tf_op jit(solution)/shard_map/all_to_all | solution.py:471
  110.5 8.5 %finish.1 = (bf16[256,4096]{1,0:T(8,128)(2,1)}, bf16[256,4096]{1,0:T(8,128)(2,1)}, f32[256,128]{1,0:T(8,128)}, f32[256,128]{1,0:T(8,128)}) custom-call(bf16[256,4096]{1,0:T(8,128)(2,1)} %x_ref.7, bf16[256,4096]{1,0:T(8,128)(2,1)} %g_ref.7, bf16[256,4096]{1,0:T(8,128)(2,1)} %get-tuple-element.29.ymix_ref, bf16[256,4096]{1,0:T(8,128)(2,1)} %get-tuple-element.30.dxmix_ref, ...), custom_call_target="tpu_custom_call" | custom-call | flops 8000000000 | bytes 16000000 | tf_op jit(solution)/shard_map/finish/pallas_call | solution.py:433
  119.1 1.1 all-to-all-done.2
  120.2 0.2 reduce_sum.9
  120.3 0.6 fusion
  (1 shorter events, 0.0 us)
Async XLA Ops:
  63.1 3.9 %copy-start.1 = (f32[4,2,16]{2,1,0:T(2,128)S(1)}, f32[4,2,16]{2,1,0:T(2,128)}, u32[]{:S(2)}) copy-start(f32[4,2,16]{2,1,0:T(2,128)} %all-gather) | copy-start | bytes 1540
  63.1 34.6 %all-to-all-start.1 = ((bf16[128,64,128]{2,1,0:T(8,128)(2,1)}), bf16[128,64,128]{2,1,0:T(8,128)(2,1)S(1)}, u32[]{:S(2)}, u32[]{:S(2)}) async-start(bf16[128,64,128]{2,1,0:T(8,128)(2,1)} %scan.1), calls=%async_computation.1 | async-start | bytes 4194304 | tf_op jit(solution)/shard_map/all_to_all | solution.py:467
  97.7 1.3 %copy-start = (bf16[128,64,128]{2,1,0:T(8,128)(2,1)}, bf16[128,64,128]{2,1,0:T(8,128)(2,1)S(1)}, u32[]{:S(2)}) copy-start(bf16[128,64,128]{2,1,0:T(8,128)(2,1)S(1)} %all-to-all-done.1.state_ref) | copy-start | bytes 6291460
  106.7 13.5 %all-to-all-start.2 = ((f32[128,1,128]{2,1,0:T(1,128)}), f32[128,1,128]{2,1,0:T(1,128)S(1)}, u32[]{:S(2)}, u32[]{:S(2)}) async-start(f32[128,1,128]{2,1,0:T(1,128)} %bitcast.14), calls=%async_computation.2 | async-start | bytes 131072 | tf_op jit(solution)/shard_map/all_to_all | solution.py:471

commit v2 on v1

--- a/solution.py
+++ b/solution.py
@@ -72,7 +72,7 @@
     return pl.BlockSpec((PARTS * lanes // WIDTH, rows, 128), lambda i: (i, 0, 0))
 
 
-def params(mib=60):
+def params(mib=62):
     return pltpu.CompilerParams(vmem_limit_bytes=mib * 1024 * 1024)
 
 
@@ -87,9 +87,13 @@
 STATES_LANES = 2048
 
 
+def heads_row(gains, row):
+    return jnp.concatenate([gains[k : k + 1] for k in range(row, gains.shape[0], 2)], axis=1)
+
+
 def states_kernel(
     place_ref, raw_ref, gains_ref, seg_ref, x_ref, g_ref, b_ref, c_ref,
-    pay_ref, scal_ref, cum2_ref, half_ref, rate_ref, row_ref,
+    pay_ref, scal_ref, cum2_ref, half_ref, rate_ref, row_ref, skip_ref,
     bt_ref, ct_ref, meta_ref,
 ):
     step = pl.program_id(0)
@@ -103,7 +107,9 @@
         high, mid, low = split3(dt)
         sums = dot(high, upto) + dot(mid, upto) + dot(low, upto)
         gains = gains_ref[...]
-        alog = jnp.concatenate([gains[k : k + 1] for k in range(0, gains.shape[0], 2)], axis=1)
+        alog = heads_row(gains, 0)
+        skip = jnp.broadcast_to(heads_row(gains, 1), (16, HEADS))
+        skip_ref[...] = jnp.concatenate(split2(skip), axis=1)
         rate = jnp.exp(jnp.broadcast_to(alog, (128, HEADS)).T)
         cum = -rate[:, :1] * sums
         tot = cum[:, BLOCK - 1 :]
@@ -118,7 +124,7 @@
         scal_ref[0] = end
         scal_ref[1] = weight
         scal_ref[2] = start
-        scal_ref[3] = dt
+        scal_ref[3] = cum
         cum2_ref[...] = cum * LOG2E
         half_ref[0] = jnp.concatenate(split2(weight), axis=0).T
         half_ref[1] = jnp.concatenate(split2(start), axis=0).T
@@ -161,11 +167,12 @@
         ],
         out_specs=[
             pieces(STATES_LANES, CARRY + META), whole(4, HEADS, BLOCK), whole(HEADS, BLOCK),
-            whole(3, BLOCK, 2 * HEADS), whole(HEADS, 128), whole(1, BLOCK),
+            whole(3, BLOCK, 2 * HEADS), whole(HEADS, 128), whole(1, BLOCK), whole(16, 2 * HEADS),
         ],
         out_shape=[
             like((PARTS, CARRY + META, 128), BF16), like((4, HEADS, BLOCK)), like((HEADS, BLOCK)),
             like((3, BLOCK, 2 * HEADS), BF16), like((HEADS, 128)), like((1, BLOCK)),
+            like((16, 2 * HEADS), BF16),
         ],
         scratch_shapes=[
             pltpu.VMEM((STATE, BLOCK), BF16),
@@ -212,7 +219,8 @@
         g_low = g_ref[:, lanes]
         x = x_low.astype(F32)
         g = g_low.astype(F32)
-        dt = dot(half_ref[2], spread(head0, 128))
+        copy = spread(head0, 128)
+        dt = dot(half_ref[2], copy)
         x_dt = (x * dt).astype(BF16)
         y = jnp.zeros((BLOCK, 128), F32)
         dx = jnp.zeros((BLOCK, 128), F32)
@@ -227,7 +235,7 @@
             total_ref[...] += dot_nt(g_one, x_dt) * kern
             y += dot(mixed, x_one)
             dx += dot_tn(mixed, g_one)
-        skip = skip_ref[:, lanes]
+        skip = dot(skip_ref[...], copy)[:1]
         gather = gather_heads(head0, 256, 128)
         y_ref[:, lanes] = (y + skip * x).astype(BF16)
         dx_ref[:, lanes] = (dx * dt + skip * g).astype(BF16)
@@ -254,7 +262,7 @@
         in_specs=[
             wide(MIX_LANES), wide(MIX_LANES), whole(BLOCK, STATE), whole(BLOCK, STATE),
             whole(1, BLOCK),
-            pl.BlockSpec((1, MIX_LANES), lambda i: (0, i)),
+            whole(16, 2 * HEADS),
             pl.BlockSpec((MIX_LANES // DIM, BLOCK), lambda i: (i, 0)),
             whole(3, BLOCK, 2 * HEADS),
         ],
@@ -318,8 +326,8 @@
     )(pay)
 
 
-def carried(state_ref, j):
-    tiles = [state_ref[k * ROWS : (k + 1) * ROWS] for k in (2 * j, 2 * j + 1)]
+def carried(state_ref):
+    tiles = [state_ref[k : k + ROWS] for k in range(0, state_ref.shape[0], ROWS)]
     h_low = jnp.concatenate([tile[:, :PIECE].reshape(STATE, 128) for tile in tiles], axis=1)
     lam_low = jnp.concatenate([tile[:, PIECE:].reshape(STATE, 128) for tile in tiles], axis=1)
     return h_low, lam_low
@@ -329,9 +337,8 @@
 
 
 def sums_kernel(
-    x_ref, g_ref, state_ref, b_ref, c_ref, scal_ref, raw_ref, rate_ref,
-    cpart_ref, ddt_ref, dskip_ref,
-    raw_grad_ref, sums_ref,
+    x_ref, g_ref, state_ref, b_ref, c_ref, scal_ref, cpart_ref, dskip_ref,
+    grads_ref, sums_ref,
     dstart_ref, dweight_ref, ddecay_ref,
 ):
     step = pl.program_id(0)
@@ -342,19 +349,22 @@
         dweight_ref[...] = jnp.zeros_like(dweight_ref)
         ddecay_ref[...] = jnp.zeros_like(ddecay_ref)
 
+    h_low, lam_low = carried(state_ref)
+    start_terms, weight_terms = [], []
     for j in range(SUMS_LANES // 256):
         lanes = slice(j * 256, (j + 1) * 256)
-        gather = gather_heads(step * (SUMS_LANES // DIM) + 4 * j, 256, 256)
-        h_low, lam_low = carried(state_ref, j)
-        from_state = dot(c_ref[...], h_low)
-        from_grad = dot(b_ref[...], lam_low)
-        dstart_ref[...] += dot((g_ref[:, lanes].astype(F32) * from_state).astype(BF16), gather)
-        dweight_ref[...] += dot((x_ref[:, lanes].astype(F32) * from_grad).astype(BF16), gather)
-        ddecay_ref[...] += dot((h_low.astype(F32) * lam_low.astype(F32)).astype(BF16), gather)
+        from_state = dot(c_ref[...], h_low[:, lanes])
+        from_grad = dot(b_ref[...], lam_low[:, lanes])
+        start_terms.append((g_ref[:, lanes].astype(F32) * from_state).astype(BF16))
+        weight_terms.append((x_ref[:, lanes].astype(F32) * from_grad).astype(BF16))
+    gather = gather_heads(step * (SUMS_LANES // DIM), SUMS_LANES, SUMS_LANES)
+    dstart_ref[...] += dot(jnp.concatenate(start_terms, axis=1), gather)
+    dweight_ref[...] += dot(jnp.concatenate(weight_terms, axis=1), gather)
+    ddecay_ref[...] += dot((h_low.astype(F32) * lam_low.astype(F32)).astype(BF16), gather)
 
     @pl.when(step == WIDTH // SUMS_LANES - 1)
     def _():
-        end, weight, start, dt = (scal_ref[k] for k in range(4))
+        weight, start, cum = (scal_ref[k] for k in (1, 2, 3))
         d_weight = dweight_ref[...].T
         used = d_weight * weight
         d_cum = cpart_ref[...] + dstart_ref[...].T * start - used
@@ -362,20 +372,14 @@
         d_decay = jnp.sum(ddecay_ref[...].T, axis=1, keepdims=True)
         d_total = jnp.sum(used, axis=1, keepdims=True) + d_decay * start[:, BLOCK - 1 :]
         d_cum = d_cum + jnp.where(at_last, d_total, 0.0)
-        square = (BLOCK, BLOCK)
-        onward = ones_where(iota(square, 0) >= iota(square, 1))
-        high, mid, low = split3(d_cum)
-        d_log = dot(high, onward) + dot(mid, onward) + dot(low, onward)
-        rate = rate_ref[:, :1]
-        d_dt = ddt_ref[...] + d_weight * end - rate * d_log
-        raw = raw_ref[...].astype(F32)
-        raw_grad_ref[...] = (d_dt / (1.0 + jnp.exp(-raw))).astype(BF16)
-        rate_grad = -jnp.sum(dt * d_log, axis=1, keepdims=True) * rate
+        grads_ref[0] = d_cum
+        grads_ref[1] = d_weight
+        rate_grad = jnp.sum(cum * d_cum, axis=1, keepdims=True)
         column = jnp.concatenate([rate_grad, dskip_ref[:, :1]], axis=0)
         sums_ref[...] = jnp.broadcast_to(column, (PARTS, 128)).T
 
 
-def gradient_sums(x, g, state, b, c, scal, raw_t, rate, cpart, ddt, dskip):
+def gradient_sums(x, g, state, b, c, scal, cpart, dskip):
     return pl.pallas_call(
         sums_kernel,
         grid=(WIDTH // SUMS_LANES,),
@@ -383,10 +387,9 @@
             wide(SUMS_LANES), wide(SUMS_LANES), pieces(SUMS_LANES, CARRY),
             whole(BLOCK, STATE), whole(BLOCK, STATE),
             whole(4, HEADS, BLOCK), whole(HEADS, BLOCK), whole(HEADS, 128),
-            whole(HEADS, BLOCK), whole(HEADS, BLOCK), whole(HEADS, 128),
-        ],
-        out_specs=[whole(HEADS, BLOCK), whole(PARTS, 128)],
-        out_shape=[like((HEADS, BLOCK), BF16), like((PARTS, 128))],
+        ],
+        out_specs=[whole(2, HEADS, BLOCK), whole(PARTS, 128)],
+        out_shape=[like((2, HEADS, BLOCK)), like((PARTS, 128))],
         scratch_shapes=[
             pltpu.VMEM((BLOCK, HEADS), F32),
             pltpu.VMEM((BLOCK, HEADS), F32),
@@ -395,7 +398,7 @@
         compiler_params=params(),
         cost_estimate=cost(10**9, 8 * 10**6, 10**5),
         name="gradient_sums",
-    )(x, g, state, b, c, scal, raw_t, rate, cpart, ddt, dskip)
+    )(x, g, state, b, c, scal, cpart, dskip)
 
 
 FINISH_LANES = 1024
@@ -403,7 +406,8 @@
 
 def finish_kernel(
     x_ref, g_ref, ymix_ref, dxmix_ref, state_ref, b_ref, c_ref, half_ref, dbmix_ref, dcmix_ref,
-    y_ref, dx_ref, db_ref, dc_ref,
+    raw_ref, rate_ref, scal_ref, grads_ref, ddt_ref,
+    y_ref, dx_ref, db_ref, dc_ref, raw_grad_ref,
 ):
     step = pl.program_id(0)
 
@@ -411,24 +415,34 @@
     def _():
         db_ref[...] = dbmix_ref[...]
         dc_ref[...] = dcmix_ref[...]
-
+        square = (BLOCK, BLOCK)
+        onward = ones_where(iota(square, 0) >= iota(square, 1))
+        high, mid, low = split3(grads_ref[0])
+        d_log = dot(high, onward) + dot(mid, onward) + dot(low, onward)
+        d_dt = ddt_ref[...] + grads_ref[1] * scal_ref[0] - rate_ref[:, :1] * d_log
+        raw = raw_ref[...].astype(F32)
+        raw_grad_ref[...] = (d_dt / (1.0 + jnp.exp(-raw))).astype(BF16)
+
+    h_low, lam_low = carried(state_ref)
+    g_scaled, x_weighted = [], []
     for j in range(FINISH_LANES // 256):
         copy = spread(step * (FINISH_LANES // DIM) + 4 * j, 256)
         lanes = slice(j * 256, (j + 1) * 256)
-        x = x_ref[:, lanes].astype(F32)
-        g = g_ref[:, lanes].astype(F32)
-        h_low, lam_low = carried(state_ref, j)
+        start = dot(half_ref[1], copy)
+        from_state = start * dot(c_ref[...], h_low[:, lanes])
+        y_ref[:, lanes] = (ymix_ref[:, lanes].astype(F32) + from_state).astype(BF16)
+        g_scaled.append((start * g_ref[:, lanes].astype(F32)).astype(BF16))
         weight = dot(half_ref[0], copy)
-        start = dot(half_ref[1], copy)
-        from_state = dot(c_ref[...], h_low)
-        from_grad = dot(b_ref[...], lam_low)
-        y_ref[:, lanes] = (ymix_ref[:, lanes].astype(F32) + start * from_state).astype(BF16)
-        dx_ref[:, lanes] = (dxmix_ref[:, lanes].astype(F32) + weight * from_grad).astype(BF16)
-        dc_ref[...] += dot_nt((start * g).astype(BF16), h_low)
-        db_ref[...] += dot_nt((weight * x).astype(BF16), lam_low)
-
-
-def finish(x, g, ymix, dxmix, state, b, c, half, dbmix, dcmix):
+        from_grad = weight * dot(b_ref[...], lam_low[:, lanes])
+        dx_ref[:, lanes] = (dxmix_ref[:, lanes].astype(F32) + from_grad).astype(BF16)
+        x_weighted.append((weight * x_ref[:, lanes].astype(F32)).astype(BF16))
+    dc_ref[...] += dot_nt(jnp.concatenate(g_scaled, axis=1), h_low)
+    db_ref[...] += dot_nt(jnp.concatenate(x_weighted, axis=1), lam_low)
+
+
+def finish(
+    x, g, ymix, dxmix, state, b, c, half, dbmix, dcmix, raw_t, rate, scal, grads, ddt
+):
     lanes = FINISH_LANES
     return pl.pallas_call(
         finish_kernel,
@@ -437,16 +451,21 @@
             wide(lanes), wide(lanes), wide(lanes), wide(lanes), pieces(lanes, CARRY),
             whole(BLOCK, STATE), whole(BLOCK, STATE),
             whole(3, BLOCK, 2 * HEADS), whole(BLOCK, STATE), whole(BLOCK, STATE),
-        ],
-        out_specs=[wide(lanes), wide(lanes), whole(BLOCK, STATE), whole(BLOCK, STATE)],
+            whole(HEADS, BLOCK), whole(HEADS, 128), whole(4, HEADS, BLOCK),
+            whole(2, HEADS, BLOCK), whole(HEADS, BLOCK),
+        ],
+        out_specs=[
+            wide(lanes), wide(lanes), whole(BLOCK, STATE), whole(BLOCK, STATE),
+            whole(HEADS, BLOCK),
+        ],
         out_shape=[
             like((BLOCK, WIDTH), BF16), like((BLOCK, WIDTH), BF16),
-            like((BLOCK, STATE)), like((BLOCK, STATE)),
+            like((BLOCK, STATE)), like((BLOCK, STATE)), like((HEADS, BLOCK), BF16),
         ],
         compiler_params=params(),
         cost_estimate=cost(8 * 10**9, 16 * 10**6, 10**5),
         name="finish",
-    )(x, g, ymix, dxmix, state, b, c, half, dbmix, dcmix)
+    )(x, g, ymix, dxmix, state, b, c, half, dbmix, dcmix, raw_t, rate, scal, grads, ddt)
 
 
 def body(inputs, dt_raw, b_proj, c_proj, a_log, d_skip, seg_ids, cotangent):
@@ -455,9 +474,8 @@
     place = mine.astype(jnp.int32).reshape(1)
     group = a_log.shape[0]
     gains = lax.all_gather(jnp.stack([a_log, d_skip]), "head", tiled=True)
-    skip = jnp.broadcast_to(gains[1::2].reshape(HEADS, 1), (HEADS, DIM)).reshape(1, WIDTH)
     raw_t = dt_raw.T
-    pay, scal, cum2, half, rate, seg = states(
+    pay, scal, cum2, half, rate, seg, skip = states(
         place, raw_t, gains, seg_ids.reshape(-1, 128), inputs, cotangent, b_proj, c_proj
     )
     pay = lax.all_to_all(pay, everyone, 0, 0, tiled=True)
@@ -465,12 +483,11 @@
         inputs, cotangent, b_proj, c_proj, seg, skip, cum2, half
     )
     state = lax.all_to_all(scan(pay), everyone, 0, 0, tiled=True)
-    raw_grad, sums = gradient_sums(
-        inputs, cotangent, state, b_proj, c_proj, scal, raw_t, rate, cpart, ddt, dskip
-    )
+    grads, sums = gradient_sums(inputs, cotangent, state, b_proj, c_proj, scal, cpart, dskip)
     sums = lax.all_to_all(sums.reshape(PARTS, 1, 128), everyone, 0, 0, tiled=True)
-    y, dx, db, dc = finish(
-        inputs, cotangent, ymix, dxmix, state, b_proj, c_proj, half, dbmix, dcmix
+    y, dx, db, dc, raw_grad = finish(
+        inputs, cotangent, ymix, dxmix, state, b_proj, c_proj, half, dbmix, dcmix,
+        raw_t, rate, scal, grads, ddt,
     )
     sums = jnp.sum(sums, axis=(0, 1))
     a_grad = lax.dynamic_slice(sums, (mine * group,), (group,))

time: 121 us -> 119 us (0.983)
  local copies, waits for them, and re-layouts: 2.79 us -> 0.59 us
    unnamed x4 -> x0, local copies, waits for them, and re-layouts: 1.33 us -> none
  transfers between devices with their start and end apart: 2 -> 2, of which waited for: 2 -> 2; matrix products, arithmetic and copies ran while one was open for 1% -> 0% of each run, Pallas kernels for 26% -> 26%
where the time goes in v2:
time: 119 us
  blocking collectives  52.9 us (44%)
  Pallas kernels  46.4 us (39%)
  waiting for transfers between devices  8.92 us (7%)
  starting transfers between devices  8.62 us (7%)
    all_to_all x1, blocking collectives, body(): pay = lax.all_to_all(pay, everyone, 0, 0, tiled=True)  44 us
    pallas_call x1, Pallas kernels, mix(): pl.pallas_call(mix_kernel, grid=(WIDTH // MIX_LANES,), in_specs=[wide(MIX...  22.6 us
    all_gather x1, blocking collectives, body(): gains = lax.all_gather(jnp.stack([a_log, d_skip]), 'head', tiled=True)  8.89 us
    pallas_call x1, Pallas kernels, finish(): pl.pallas_call(finish_kernel, grid=(WIDTH // lanes,), in_specs=[wide(lane...  8.44 us
    all_to_all x1, waiting for transfers between devices, body(): state = lax.all_to_all(scan(pay), everyone, 0, 0, tiled=True)  7.76 us
    pallas_call x1, Pallas kernels, gradient_sums(): pl.pallas_call(sums_kernel, grid=(WIDTH // SUMS_LANES,), in_specs=[wide(S...  6.53 us
    pallas_call x1, Pallas kernels, states(): pl.pallas_call(states_kernel, grid=(WIDTH // STATES_LANES,), in_specs=[pl...  5.29 us
    all_to_all x1, starting transfers between devices, body(): state = lax.all_to_all(scan(pay), everyone, 0, 0, tiled=True)  4.81 us
  transfers between devices with their start and end apart: 2, of which 2 were waited for; matrix products, arithmetic and copies ran while one was open for 0% of the time, Pallas kernels for 26%

profile of v2, /device:TPU:1, one launch (start us, length us, event | category | flops | bytes accessed | tf_op | source)
XLA Modules:
  0.0 119.0 jit_solution(15706633255059379593)
XLA Ops:
  0.6 0.7 maximum_bitcast_fusion
  1.3 8.9 %all-gather = f32[4,2,16]{2,1,0:T(2,128)} all-gather(f32[1,2,16]{2,1,0:T(2,128)S(1)} %maximum_bitcast_fusion), channel_id=1, replica_groups=mesh['head'=4,'seq'=32] {'head'}, dimensions={0}, use_global_device_ids=true | all-gather | bytes 640 | tf_op jit(solution)/shard_map/all_gather | solution.py:476
  10.2 5.3 %states.1 = (bf16[128,72,128]{2,1,0:T(8,128)(2,1)}, f32[4,64,256]{2,1,0:T(8,128)}, f32[64,256]{1,0:T(8,128)}, bf16[3,256,128]{2,1,0:T(8,128)(2,1)}, f32[64,128]{...) custom-call(s32[1]{0:T(128)} %bitcast.place_ref, bf16[64,256]{1,0:T(8,128)(2,1)} %bitcast.13, f32[8,16]{1,0:T(8,128)} %bitcast.15, ...), custom_call_target="tpu_custom_call" | custom-call | flops 1000000000 | bytes 8000000 | tf_op jit(solution)/shard_map/states/pallas_call | solution.py:160
  15.5 44.0 %all_to_all.15.pay_ref = bf16[128,72,128]{2,1,0:T(8,128)(2,1)S(1)} all-to-all(bf16[128,72,128]{2,1,0:T(8,128)(2,1)} %get-tuple-element.34), channel_id=1, replica_groups=mesh['head'=4,'seq'=32] {'seq','head'}, dimensions={0} | all-to-all | bytes 4718592 | tf_op jit(solution)/shard_map/all_to_all | solution.py:481
  59.5 3.6 %scan.1 = bf16[128,64,128]{2,1,0:T(8,128)(2,1)} custom-call(bf16[128,72,128]{2,1,0:T(8,128)(2,1)S(1)} %all_to_all.15.pay_ref), custom_call_target="tpu_custom_call" | custom-call | flops 500000000 | bytes 5000000 | tf_op jit(solution)/shard_map/scan/pallas_call | solution.py:318
  63.1 4.8 %all-to-all-start.1 = ((bf16[128,64,128]{2,1,0:T(8,128)(2,1)}), bf16[128,64,128]{2,1,0:T(8,128)(2,1)}, u32[]{:S(2)}, u32[]{:S(2)}) async-start(bf16[128,64,128]{2,1,0:T(8,128)(2,1)} %scan.1), calls=%async_computation.1 | async-start | bytes 4194304 | tf_op jit(solution)/shard_map/all_to_all | solution.py:485
  67.9 22.6 %mix.1 = (bf16[256,4096]{1,0:T(8,128)(2,1)}, bf16[256,4096]{1,0:T(8,128)(2,1)}, f32[64,256]{1,0:T(8,128)}, f32[64,256]{1,0:T(8,128)}, f32[256,128]{1,0:T(8,128)}, /*index=5*/f32[256,128]{1,0:T(8,128)}, f32[64,128]{1,0:T(8,128)}) custom-call(bf16[256,4096]{1,0:T(8,128)(2,1)} %x_ref.7, bf16[256,4096]{1,0:T(8,128)(2,1)} %g_ref.7, bf16[256,128]{1,0:T(8,128)(2,1)} %b_ref.7, ...), custom_call_target="tpu_custom_call" | custom-call | flops 20000000000 | bytes 9000000 | tf_op jit(solution)/shard_map/mix/pallas_call | solution.py:259
  90.5 7.8 %all-to-all-done.1.state_ref = bf16[128,64,128]{2,1,0:T(8,128)(2,1)} async-done(((bf16[128,64,128]{2,1,0:T(8,128)(2,1)}), bf16[128,64,128]{2,1,0:T(8,128)(2,1)}, u32[]{:S(2)}, u32[]{:S(2)}) %all-to-all-start.1) | async-done | bytes 2097184 | tf_op jit(solution)/shard_map/all_to_all | solution.py:485
  98.3 6.5 %gradient_sums.1 = (f32[2,64,256]{2,1,0:T(8,128)}, f32[128,128]{1,0:T(8,128)}) custom-call(bf16[256,4096]{1,0:T(8,128)(2,1)} %x_ref.7, bf16[256,4096]{1,0:T(8,128)(2,1)} %g_ref.7, bf16[128,64,128]{2,1,0:T(8,128)(2,1)} %all-to-all-done.1.state_ref, bf16[256,128]{1,0:T(8,128)(2,1)} %b_ref.7, bf16[256,128]{1,0:T(8,128)(2,1)} %c_ref.7, ...), custom_call_target="tpu_custom_call" | custom-call | flops 1000000000 | bytes 8000000 | tf_op jit(solution)/shard_map/gradient_sums/pallas_call | solution.py:383
  104.8 3.8 %all-to-all-start.2 = ((f32[128,1,128]{2,1,0:T(1,128)}), f32[128,1,128]{2,1,0:T(1,128)S(1)}, u32[]{:S(2)}, u32[]{:S(2)}) async-start(f32[128,1,128]{2,1,0:T(1,128)} %bitcast.12), calls=%async_computation.2 | async-start | bytes 131072 | tf_op jit(solution)/shard_map/all_to_all | solution.py:487
  108.6 8.4 %finish.1 = (bf16[256,4096]{1,0:T(8,128)(2,1)}, bf16[256,4096]{1,0:T(8,128)(2,1)}, f32[256,128]{1,0:T(8,128)}, f32[256,128]{1,0:T(8,128)}, bf16[64,256]{1,0:T(8,128)(2,1)}) custom-call(bf16[256,4096]{1,0:T(8,128)(2,1)} %x_ref.7, bf16[256,4096]{1,0:T(8,128)(2,1)} %g_ref.7, bf16[256,4096]{1,0:T(8,128)(2,1)} %get-tuple-element.32.ymix_ref, ...), custom_call_target="tpu_custom_call" | custom-call | flops 8000000000 | bytes 16000000 | tf_op jit(solution)/shard_map/finish/pallas_call | solution.py:447
  117.1 1.2 all-to-all-done.2
  118.2 0.2 reduce_sum.9
  118.4 0.6 fusion
Async XLA Ops:
  63.1 35.2 %all-to-all-start.1 = ((bf16[128,64,128]{2,1,0:T(8,128)(2,1)}), bf16[128,64,128]{2,1,0:T(8,128)(2,1)}, u32[]{:S(2)}, u32[]{:S(2)}) async-start(bf16[128,64,128]{2,1,0:T(8,128)(2,1)} %scan.1), calls=%async_computation.1 | async-start | bytes 4194304 | tf_op jit(solution)/shard_map/all_to_all | solution.py:485
  104.8 13.4 %all-to-all-start.2 = ((f32[128,1,128]{2,1,0:T(1,128)}), f32[128,1,128]{2,1,0:T(1,128)S(1)}, u32[]{:S(2)}, u32[]{:S(2)}) async-start(f32[128,1,128]{2,1,0:T(1,128)} %bitcast.12), calls=%async_computation.2 | async-start | bytes 131072 | tf_op jit(solution)/shard_map/all_to_all | solution.py:487

commit v3 on v2

--- a/solution.py
+++ b/solution.py
@@ -66,6 +66,10 @@
 
 def wide(lanes):
     return pl.BlockSpec((BLOCK, lanes), lambda i: (0, i))
+
+
+def moment(lanes):
+    return pl.BlockSpec((STATE, lanes), lambda i: (0, i))
 
 
 def pieces(lanes, rows):
@@ -129,6 +133,8 @@
         half_ref[0] = jnp.concatenate(split2(weight), axis=0).T
         half_ref[1] = jnp.concatenate(split2(start), axis=0).T
         half_ref[2] = jnp.concatenate(split2(dt), axis=0).T
+        half_ref[3] = jnp.concatenate(split2(cum * start), axis=0).T
+        half_ref[4] = jnp.concatenate(split2((tot - cum) * weight), axis=0).T
         rate_ref[...] = rate
         row_ref[...] = seg
         bt_ref[...] = b_ref[...].T
@@ -167,11 +173,11 @@
         ],
         out_specs=[
             pieces(STATES_LANES, CARRY + META), whole(4, HEADS, BLOCK), whole(HEADS, BLOCK),
-            whole(3, BLOCK, 2 * HEADS), whole(HEADS, 128), whole(1, BLOCK), whole(16, 2 * HEADS),
+            whole(5, BLOCK, 2 * HEADS), whole(HEADS, 128), whole(1, BLOCK), whole(16, 2 * HEADS),
         ],
         out_shape=[
             like((PARTS, CARRY + META, 128), BF16), like((4, HEADS, BLOCK)), like((HEADS, BLOCK)),
-            like((3, BLOCK, 2 * HEADS), BF16), like((HEADS, 128)), like((1, BLOCK)),
+            like((5, BLOCK, 2 * HEADS), BF16), like((HEADS, 128)), like((1, BLOCK)),
             like((16, 2 * HEADS), BF16),
         ],
         scratch_shapes=[
@@ -185,13 +191,15 @@
     )(place, raw_t, gains, seg_ids, x, g, b, c)
 
 
-MIX_LANES = 512
+MIX_LANES = 1024
+HALF = BLOCK // 2
 
 
 def mix_kernel(
     x_ref, g_ref, b_ref, c_ref, seg_ref, skip_ref, cum2_ref, half_ref,
-    y_ref, dx_ref, cpart_ref, ddt_ref, db_ref, dc_ref, dskip_ref,
+    y_ref, dx_ref, cpart_ref, ddt_ref, db_ref, dc_ref, dskip_ref, start_mom_ref, end_mom_ref,
     gram_ref, mask_ref, total_ref, cpart_sum_ref, ddt_sum_ref, dskip_sum_ref,
+    bt_ref, ct_ref,
 ):
     step = pl.program_id(0)
     square = (BLOCK, BLOCK)
@@ -207,7 +215,14 @@
         cpart_sum_ref[...] = jnp.zeros_like(cpart_sum_ref)
         ddt_sum_ref[...] = jnp.zeros_like(ddt_sum_ref)
         dskip_sum_ref[...] = jnp.zeros_like(dskip_sum_ref)
-
+        bt_ref[...] = b_ref[...].T
+        ct_ref[...] = c_ref[...].T
+
+    copy = spread(step * (MIX_LANES // DIM), MIX_LANES)
+    g_moment = (g_ref[...].astype(F32) * dot(half_ref[3], copy)).astype(BF16)
+    start_mom_ref[...] = dot(ct_ref[...], g_moment).astype(BF16)
+    x_moment = (x_ref[...].astype(F32) * dot(half_ref[4], copy)).astype(BF16)
+    end_mom_ref[...] = dot(bt_ref[...], x_moment).astype(BF16)
     lower = iota((BLOCK, 128), 1) < DIM
     zero = jnp.zeros((BLOCK, 128), BF16)
     cum2 = cum2_ref[...]
@@ -222,19 +237,22 @@
         copy = spread(head0, 128)
         dt = dot(half_ref[2], copy)
         x_dt = (x * dt).astype(BF16)
-        y = jnp.zeros((BLOCK, 128), F32)
-        dx = jnp.zeros((BLOCK, 128), F32)
+        ys = [jnp.zeros((HALF, 128), F32)] * 2
+        dxs = [jnp.zeros((HALF, 128), F32), jnp.zeros((BLOCK, 128), F32)]
         for k in range(2):
             pick = lower if k == 0 else ~lower
             g_one = jnp.where(pick, g_low, zero)
             x_one = jnp.where(pick, x_dt, zero)
             head = 2 * j + k
-            gap = columns[:, head : head + 1] - cum2[head : head + 1, :]
-            kern = jnp.exp2(gap + mask_ref[...])
-            mixed = (gram_ref[...] * kern).astype(BF16)
-            total_ref[...] += dot_nt(g_one, x_dt) * kern
-            y += dot(mixed, x_one)
-            dx += dot_tn(mixed, g_one)
+            col, row = columns[:, head : head + 1], cum2[head : head + 1, :]
+            for rows, upto in ((slice(0, HALF), HALF), (slice(HALF, BLOCK), BLOCK)):
+                kern = jnp.exp2(col[rows] - row[:, :upto] + mask_ref[rows, :upto])
+                mixed = (gram_ref[rows, :upto] * kern).astype(BF16)
+                total_ref[rows, :upto] += dot_nt(g_one[rows], x_dt[:upto]) * kern
+                ys[rows.start // HALF] += dot(mixed, x_one[:upto])
+                dxs[rows.start // HALF] += dot_tn(mixed, g_one[rows])
+        y = jnp.concatenate(ys, axis=0)
+        dx = jnp.concatenate([dxs[0] + dxs[1][:HALF], dxs[1][HALF:]], axis=0)
         skip = dot(skip_ref[...], copy)[:1]
         gather = gather_heads(head0, 256, 128)
         y_ref[:, lanes] = (y + skip * x).astype(BF16)
@@ -264,20 +282,23 @@
             whole(1, BLOCK),
             whole(16, 2 * HEADS),
             pl.BlockSpec((MIX_LANES // DIM, BLOCK), lambda i: (i, 0)),
-            whole(3, BLOCK, 2 * HEADS),
+            whole(5, BLOCK, 2 * HEADS),
         ],
         out_specs=[
             wide(MIX_LANES), wide(MIX_LANES), whole(HEADS, BLOCK), whole(HEADS, BLOCK),
             whole(BLOCK, STATE), whole(BLOCK, STATE), whole(HEADS, 128),
+            moment(MIX_LANES), moment(MIX_LANES),
         ],
         out_shape=[
             like((BLOCK, WIDTH), BF16), like((BLOCK, WIDTH), BF16),
             like((HEADS, BLOCK)), like((HEADS, BLOCK)),
             like((BLOCK, STATE)), like((BLOCK, STATE)), like((HEADS, 128)),
+            like((STATE, WIDTH), BF16), like((STATE, WIDTH), BF16),
         ],
         scratch_shapes=[pltpu.VMEM((BLOCK, BLOCK), F32)] * 3
         + [pltpu.VMEM((BLOCK, HEADS), F32)] * 2
-        + [pltpu.VMEM((8, HEADS), F32)],
+        + [pltpu.VMEM((8, HEADS), F32)]
+        + [pltpu.VMEM((STATE, BLOCK), BF16)] * 2,
         compiler_params=params(),
         cost_estimate=cost(20 * 10**9, 9 * 10**6, 4 * 10**6),
         name="mix",
@@ -337,68 +358,58 @@
 
 
 def sums_kernel(
-    x_ref, g_ref, state_ref, b_ref, c_ref, scal_ref, cpart_ref, dskip_ref,
-    grads_ref, sums_ref,
-    dstart_ref, dweight_ref, ddecay_ref,
+    start_mom_ref, end_mom_ref, state_ref, scal_ref, cpart_ref, dskip_ref,
+    ddecay_ref, sums_ref,
+    total_ref,
 ):
     step = pl.program_id(0)
 
     @pl.when(step == 0)
     def _():
-        dstart_ref[...] = jnp.zeros_like(dstart_ref)
-        dweight_ref[...] = jnp.zeros_like(dweight_ref)
-        ddecay_ref[...] = jnp.zeros_like(ddecay_ref)
+        total_ref[...] = jnp.zeros_like(total_ref)
 
     h_low, lam_low = carried(state_ref)
-    start_terms, weight_terms = [], []
-    for j in range(SUMS_LANES // 256):
-        lanes = slice(j * 256, (j + 1) * 256)
-        from_state = dot(c_ref[...], h_low[:, lanes])
-        from_grad = dot(b_ref[...], lam_low[:, lanes])
-        start_terms.append((g_ref[:, lanes].astype(F32) * from_state).astype(BF16))
-        weight_terms.append((x_ref[:, lanes].astype(F32) * from_grad).astype(BF16))
+    h = h_low.astype(F32)
+    lam = lam_low.astype(F32)
+    moments = h * start_mom_ref[...].astype(F32) + lam * end_mom_ref[...].astype(F32)
+    moments = jnp.sum(moments, axis=0, keepdims=True)
+    inner = jnp.sum(h * lam, axis=0, keepdims=True)
+    kind = iota((16, SUMS_LANES), 0)
+    rows = jnp.where(kind == 0, moments, jnp.where(kind == 1, inner, 0.0))
     gather = gather_heads(step * (SUMS_LANES // DIM), SUMS_LANES, SUMS_LANES)
-    dstart_ref[...] += dot(jnp.concatenate(start_terms, axis=1), gather)
-    dweight_ref[...] += dot(jnp.concatenate(weight_terms, axis=1), gather)
-    ddecay_ref[...] += dot((h_low.astype(F32) * lam_low.astype(F32)).astype(BF16), gather)
+    high, low = split2(rows)
+    total_ref[...] += dot(high, gather) + dot(low, gather)
 
     @pl.when(step == WIDTH // SUMS_LANES - 1)
     def _():
-        weight, start, cum = (scal_ref[k] for k in (1, 2, 3))
-        d_weight = dweight_ref[...].T
-        used = d_weight * weight
-        d_cum = cpart_ref[...] + dstart_ref[...].T * start - used
-        at_last = iota((HEADS, BLOCK), 1) == BLOCK - 1
-        d_decay = jnp.sum(ddecay_ref[...].T, axis=1, keepdims=True)
-        d_total = jnp.sum(used, axis=1, keepdims=True) + d_decay * start[:, BLOCK - 1 :]
-        d_cum = d_cum + jnp.where(at_last, d_total, 0.0)
-        grads_ref[0] = d_cum
-        grads_ref[1] = d_weight
-        rate_grad = jnp.sum(cum * d_cum, axis=1, keepdims=True)
+        total = jnp.concatenate(
+            [total_ref[...], jnp.zeros((128 - 16, HEADS), F32)], axis=0
+        ).T
+        d_decay = total[:, 1:2]
+        start, cum = scal_ref[2], scal_ref[3]
+        at_end = cum[:, BLOCK - 1 :] * start[:, BLOCK - 1 :]
+        inside = jnp.sum(cum * cpart_ref[...], axis=1, keepdims=True)
+        rate_grad = inside + total[:, :1] + at_end * d_decay
+        ddecay_ref[...] = jnp.broadcast_to(d_decay, (HEADS, 128))
         column = jnp.concatenate([rate_grad, dskip_ref[:, :1]], axis=0)
         sums_ref[...] = jnp.broadcast_to(column, (PARTS, 128)).T
 
 
-def gradient_sums(x, g, state, b, c, scal, cpart, dskip):
+def gradient_sums(start_mom, end_mom, state, scal, cpart, dskip):
     return pl.pallas_call(
         sums_kernel,
         grid=(WIDTH // SUMS_LANES,),
         in_specs=[
-            wide(SUMS_LANES), wide(SUMS_LANES), pieces(SUMS_LANES, CARRY),
-            whole(BLOCK, STATE), whole(BLOCK, STATE),
+            moment(SUMS_LANES), moment(SUMS_LANES), pieces(SUMS_LANES, CARRY),
             whole(4, HEADS, BLOCK), whole(HEADS, BLOCK), whole(HEADS, 128),
         ],
-        out_specs=[whole(2, HEADS, BLOCK), whole(PARTS, 128)],
-        out_shape=[like((2, HEADS, BLOCK)), like((PARTS, 128))],
-        scratch_shapes=[
-            pltpu.VMEM((BLOCK, HEADS), F32),
-            pltpu.VMEM((BLOCK, HEADS), F32),
-            pltpu.VMEM((STATE, HEADS), F32),
-        ],
+        out_specs=[whole(HEADS, 128), whole(PARTS, 128)],
+        out_shape=[like((HEADS, 128)), like((PARTS, 128))],
+        scratch_shapes=[pltpu.VMEM((16, HEADS), F32)],
         compiler_params=params(),
-        cost_estimate=cost(10**9, 8 * 10**6, 10**5),
+        cost_estimate=cost(10**8, 4 * 10**6, 10**4),
         name="gradient_sums",
-    )(x, g, state, b, c, scal, cpart, dskip)
+    )(start_mom, end_mom, state, scal, cpart, dskip)
 
 
 FINISH_LANES = 1024
@@ -406,8 +417,9 @@
 
 def finish_kernel(
     x_ref, g_ref, ymix_ref, dxmix_ref, state_ref, b_ref, c_ref, half_ref, dbmix_ref, dcmix_ref,
-    raw_ref, rate_ref, scal_ref, grads_ref, ddt_ref,
+    raw_ref, rate_ref, scal_ref, cpart_ref, ddecay_ref, ddt_ref,
     y_ref, dx_ref, db_ref, dc_ref, raw_grad_ref,
+    dstart_ref, dweight_ref,
 ):
     step = pl.program_id(0)
 
@@ -415,33 +427,54 @@
     def _():
         db_ref[...] = dbmix_ref[...]
         dc_ref[...] = dcmix_ref[...]
-        square = (BLOCK, BLOCK)
-        onward = ones_where(iota(square, 0) >= iota(square, 1))
-        high, mid, low = split3(grads_ref[0])
-        d_log = dot(high, onward) + dot(mid, onward) + dot(low, onward)
-        d_dt = ddt_ref[...] + grads_ref[1] * scal_ref[0] - rate_ref[:, :1] * d_log
-        raw = raw_ref[...].astype(F32)
-        raw_grad_ref[...] = (d_dt / (1.0 + jnp.exp(-raw))).astype(BF16)
+        dstart_ref[...] = jnp.zeros_like(dstart_ref)
+        dweight_ref[...] = jnp.zeros_like(dweight_ref)
 
     h_low, lam_low = carried(state_ref)
-    g_scaled, x_weighted = [], []
+    g_scaled, x_weighted, start_terms, weight_terms = [], [], [], []
     for j in range(FINISH_LANES // 256):
         copy = spread(step * (FINISH_LANES // DIM) + 4 * j, 256)
         lanes = slice(j * 256, (j + 1) * 256)
         start = dot(half_ref[1], copy)
+        g = g_ref[:, lanes].astype(F32)
         from_state = start * dot(c_ref[...], h_low[:, lanes])
+        start_terms.append((g * from_state).astype(BF16))
         y_ref[:, lanes] = (ymix_ref[:, lanes].astype(F32) + from_state).astype(BF16)
-        g_scaled.append((start * g_ref[:, lanes].astype(F32)).astype(BF16))
+        g_scaled.append((start * g).astype(BF16))
         weight = dot(half_ref[0], copy)
-        from_grad = weight * dot(b_ref[...], lam_low[:, lanes])
+        x = x_ref[:, lanes].astype(F32)
+        plain_grad = dot(b_ref[...], lam_low[:, lanes])
+        weight_terms.append((x * plain_grad).astype(BF16))
+        from_grad = weight * plain_grad
         dx_ref[:, lanes] = (dxmix_ref[:, lanes].astype(F32) + from_grad).astype(BF16)
-        x_weighted.append((weight * x_ref[:, lanes].astype(F32)).astype(BF16))
+        x_weighted.append((weight * x).astype(BF16))
     dc_ref[...] += dot_nt(jnp.concatenate(g_scaled, axis=1), h_low)
     db_ref[...] += dot_nt(jnp.concatenate(x_weighted, axis=1), lam_low)
+    gather = gather_heads(step * (FINISH_LANES // DIM), FINISH_LANES, FINISH_LANES)
+    dstart_ref[...] += dot(jnp.concatenate(start_terms, axis=1), gather)
+    dweight_ref[...] += dot(jnp.concatenate(weight_terms, axis=1), gather)
+
+    @pl.when(step == WIDTH // FINISH_LANES - 1)
+    def _():
+        end, weight, start = (scal_ref[k] for k in range(3))
+        d_weight = dweight_ref[...].T
+        used = d_weight * weight
+        d_cum = cpart_ref[...] + dstart_ref[...].T - used
+        at_last = iota((HEADS, BLOCK), 1) == BLOCK - 1
+        d_total = jnp.sum(used, axis=1, keepdims=True)
+        d_total = d_total + ddecay_ref[:, :1] * start[:, BLOCK - 1 :]
+        d_cum = d_cum + jnp.where(at_last, d_total, 0.0)
+        square = (BLOCK, BLOCK)
+        onward = ones_where(iota(square, 0) >= iota(square, 1))
+        high, mid, low = split3(d_cum)
+        d_log = dot(high, onward) + dot(mid, onward) + dot(low, onward)
+        d_dt = ddt_ref[...] + d_weight * end - rate_ref[:, :1] * d_log
+        raw = raw_ref[...].astype(F32)
+        raw_grad_ref[...] = (d_dt / (1.0 + jnp.exp(-raw))).astype(BF16)
 
 
 def finish(
-    x, g, ymix, dxmix, state, b, c, half, dbmix, dcmix, raw_t, rate, scal, grads, ddt
+    x, g, ymix, dxmix, state, b, c, half, dbmix, dcmix, raw_t, rate, scal, cpart, ddecay, ddt
 ):
     lanes = FINISH_LANES
     return pl.pallas_call(
@@ -450,9 +483,9 @@
         in_specs=[
             wide(lanes), wide(lanes), wide(lanes), wide(lanes), pieces(lanes, CARRY),
             whole(BLOCK, STATE), whole(BLOCK, STATE),
-            whole(3, BLOCK, 2 * HEADS), whole(BLOCK, STATE), whole(BLOCK, STATE),
+            whole(5, BLOCK, 2 * HEADS), whole(BLOCK, STATE), whole(BLOCK, STATE),
             whole(HEADS, BLOCK), whole(HEADS, 128), whole(4, HEADS, BLOCK),
-            whole(2, HEADS, BLOCK), whole(HEADS, BLOCK),
+            whole(HEADS, BLOCK), whole(HEADS, 128), whole(HEADS, BLOCK),
         ],
         out_specs=[
             wide(lanes), wide(lanes), whole(BLOCK, STATE), whole(BLOCK, STATE),
@@ -462,10 +495,11 @@
             like((BLOCK, WIDTH), BF16), like((BLOCK, WIDTH), BF16),
             like((BLOCK, STATE)), like((BLOCK, STATE)), like((HEADS, BLOCK), BF16),
         ],
+        scratch_shapes=[pltpu.VMEM((BLOCK, HEADS), F32)] * 2,
         compiler_params=params(),
         cost_estimate=cost(8 * 10**9, 16 * 10**6, 10**5),
         name="finish",
-    )(x, g, ymix, dxmix, state, b, c, half, dbmix, dcmix, raw_t, rate, scal, grads, ddt)
+    )(x, g, ymix, dxmix, state, b, c, half, dbmix, dcmix, raw_t, rate, scal, cpart, ddecay, ddt)
 
 
 def body(inputs, dt_raw, b_proj, c_proj, a_log, d_skip, seg_ids, cotangent):
@@ -479,15 +513,15 @@
         place, raw_t, gains, seg_ids.reshape(-1, 128), inputs, cotangent, b_proj, c_proj
     )
     pay = lax.all_to_all(pay, everyone, 0, 0, tiled=True)
-    ymix, dxmix, cpart, ddt, dbmix, dcmix, dskip = mix(
+    ymix, dxmix, cpart, ddt, dbmix, dcmix, dskip, start_mom, end_mom = mix(
         inputs, cotangent, b_proj, c_proj, seg, skip, cum2, half
     )
     state = lax.all_to_all(scan(pay), everyone, 0, 0, tiled=True)
-    grads, sums = gradient_sums(inputs, cotangent, state, b_proj, c_proj, scal, cpart, dskip)
+    ddecay, sums = gradient_sums(start_mom, end_mom, state, scal, cpart, dskip)
     sums = lax.all_to_all(sums.reshape(PARTS, 1, 128), everyone, 0, 0, tiled=True)
     y, dx, db, dc, raw_grad = finish(
         inputs, cotangent, ymix, dxmix, state, b_proj, c_proj, half, dbmix, dcmix,
-        raw_t, rate, scal, grads, ddt,
+        raw_t, rate, scal, cpart, ddecay, ddt,
     )
     sums = jnp.sum(sums, axis=(0, 1))
     a_grad = lax.dynamic_slice(sums, (mine * group,), (group,))

time: 119 us -> 118 us (level)
  Pallas kernels: 46.4 us -> 44.6 us
    pallas_call x1, Pallas kernels: 6.53 us -> 4.61 us  [gradient_sums(): pl.pallas_call(sums_kernel, grid=(WIDTH // SUMS_LANES,), in_specs=[moment...]
    pallas_call x1, Pallas kernels: 8.44 us -> 10.1 us  [finish(): pl.pallas_call(finish_kernel, grid=(WIDTH // lanes,), in_specs=[wide(lane...]
    all_to_all x1, waiting for transfers between devices: 7.76 us -> 9.4 us  [body(): state = lax.all_to_all(scan(pay), everyone, 0, 0, tiled=True)]
    pallas_call x1, Pallas kernels: 22.6 us -> 20.9 us  [mix(): pl.pallas_call(mix_kernel, grid=(WIDTH // MIX_LANES,), in_specs=[wide(MIX...]
  transfers between devices with their start and end apart: 2 -> 2, of which waited for: 2 -> 1; matrix products, arithmetic and copies ran while one was open for 0% -> 0% of each run, Pallas kernels for 26% -> 26%
where the time goes in v3:
time: 118 us
  blocking collectives  52.9 us (45%)
  Pallas kernels  44.6 us (38%)
  waiting for transfers between devices  9.41 us (8%)
  starting transfers between devices  8.62 us (7%)
    all_to_all x1, blocking collectives, body(): pay = lax.all_to_all(pay, everyone, 0, 0, tiled=True)  44 us
    pallas_call x1, Pallas kernels, mix(): pl.pallas_call(mix_kernel, grid=(WIDTH // MIX_LANES,), in_specs=[wide(MIX...  20.9 us
    pallas_call x1, Pallas kernels, finish(): pl.pallas_call(finish_kernel, grid=(WIDTH // lanes,), in_specs=[wide(lane...  10.1 us
    all_to_all x1, waiting for transfers between devices, body(): state = lax.all_to_all(scan(pay), everyone, 0, 0, tiled=True)  9.4 us
    all_gather x1, blocking collectives, body(): gains = lax.all_gather(jnp.stack([a_log, d_skip]), 'head', tiled=True)  8.89 us
    pallas_call x1, Pallas kernels, states(): pl.pallas_call(states_kernel, grid=(WIDTH // STATES_LANES,), in_specs=[pl...  5.34 us
    all_to_all x1, starting transfers between devices, body(): state = lax.all_to_all(scan(pay), everyone, 0, 0, tiled=True)  4.8 us
    pallas_call x1, Pallas kernels, gradient_sums(): pl.pallas_call(sums_kernel, grid=(WIDTH // SUMS_LANES,), in_specs=[moment...  4.61 us
  transfers between devices with their start and end apart: 2, of which 1 were waited for; matrix products, arithmetic and copies ran while one was open for 0% of the time, Pallas kernels for 26%

profile of v3, /device:TPU:1, one launch (start us, length us, event | category | flops | bytes accessed | tf_op | source)
XLA Modules:
  0.0 117.6 jit_solution(5042840657655785075)
XLA Ops:
  0.6 0.7 maximum_bitcast_fusion
  1.3 8.9 %all-gather = f32[4,2,16]{2,1,0:T(2,128)} all-gather(f32[1,2,16]{2,1,0:T(2,128)S(1)} %maximum_bitcast_fusion), channel_id=1, replica_groups=mesh['head'=4,'seq'=32] {'head'}, dimensions={0}, use_global_device_ids=true | all-gather | bytes 640 | tf_op jit(solution)/shard_map/all_gather | solution.py:510
  10.2 5.3 %states.1 = (bf16[128,72,128]{2,1,0:T(8,128)(2,1)}, f32[4,64,256]{2,1,0:T(8,128)}, f32[64,256]{1,0:T(8,128)}, bf16[5,256,128]{2,1,0:T(8,128)(2,1)}, f32[64,128]{...) custom-call(s32[1]{0:T(128)} %bitcast.place_ref, bf16[64,256]{1,0:T(8,128)(2,1)} %bitcast.13, f32[8,16]{1,0:T(8,128)} %bitcast.15, ...), custom_call_target="tpu_custom_call" | custom-call | flops 1000000000 | bytes 8000000 | tf_op jit(solution)/shard_map/states/pallas_call | solution.py:166
  15.6 44.0 %all_to_all.15.pay_ref = bf16[128,72,128]{2,1,0:T(8,128)(2,1)S(1)} all-to-all(bf16[128,72,128]{2,1,0:T(8,128)(2,1)} %get-tuple-element.36), channel_id=1, replica_groups=mesh['head'=4,'seq'=32] {'seq','head'}, dimensions={0} | all-to-all | bytes 4718592 | tf_op jit(solution)/shard_map/all_to_all | solution.py:515
  59.6 3.6 %scan.1 = bf16[128,64,128]{2,1,0:T(8,128)(2,1)} custom-call(bf16[128,72,128]{2,1,0:T(8,128)(2,1)S(1)} %all_to_all.15.pay_ref), custom_call_target="tpu_custom_call" | custom-call | flops 500000000 | bytes 5000000 | tf_op jit(solution)/shard_map/scan/pallas_call | solution.py:339
  63.1 4.8 %all-to-all-start.1 = ((bf16[128,64,128]{2,1,0:T(8,128)(2,1)}), bf16[128,64,128]{2,1,0:T(8,128)(2,1)}, u32[]{:S(2)}, u32[]{:S(2)}) async-start(bf16[128,64,128]{2,1,0:T(8,128)(2,1)} %scan.1), calls=%async_computation.1 | async-start | bytes 4194304 | tf_op jit(solution)/shard_map/all_to_all | solution.py:519
  68.0 20.9 %mix.1 = (bf16[256,4096]{1,0:T(8,128)(2,1)}, bf16[256,4096]{1,0:T(8,128)(2,1)}, f32[64,256]{1,0:T(8,128)}, f32[64,256]{1,0:T(8,128)}, f32[256,128]{1,0:T(8,128)}...) custom-call(bf16[256,4096]{1,0:T(8,128)(2,1)} %x_ref.5, ...), custom_call_target="tpu_custom_call" | custom-call | flops 20000000000 | bytes 9000000 | tf_op jit(solution)/shard_map/mix/pallas_call | solution.py:277
  88.9 9.4 %all-to-all-done.1.state_ref = bf16[128,64,128]{2,1,0:T(8,128)(2,1)} async-done(((bf16[128,64,128]{2,1,0:T(8,128)(2,1)}), bf16[128,64,128]{2,1,0:T(8,128)(2,1)}, u32[]{:S(2)}, u32[]{:S(2)}) %all-to-all-start.1) | async-done | bytes 2097184 | tf_op jit(solution)/shard_map/all_to_all | solution.py:519
  98.3 4.6 %gradient_sums.1 = (f32[64,128]{1,0:T(8,128)}, f32[128,128]{1,0:T(8,128)}) custom-call(bf16[128,4096]{1,0:T(8,128)(2,1)} %get-tuple-element.42.start_mom_ref, bf16[128,4096]{1,0:T(8,128)(2,1)} %get-tuple-element.43.end_mom_ref, bf16[128,64,128]{2,1,0:T(8,128)(2,1)} %all-to-all-done.1.state_ref, f32[4,64,256]{2,1,0:T(8,128)} %get-tuple-element.40.scal_ref, ...), custom_call_target="tpu_custom_call" | custom-call | flops 100000000 | bytes 4000000 | tf_op jit(solution)/shard_map/gradient_sums/pallas_call | solution.py:399
  102.9 3.8 %all-to-all-start.2 = ((f32[128,1,128]{2,1,0:T(1,128)}), f32[128,1,128]{2,1,0:T(1,128)S(1)}, u32[]{:S(2)}, u32[]{:S(2)}) async-start(f32[128,1,128]{2,1,0:T(1,128)} %bitcast.12), calls=%async_computation.2 | async-start | bytes 131072 | tf_op jit(solution)/shard_map/all_to_all | solution.py:521
  106.7 10.1 %finish.1 = (bf16[256,4096]{1,0:T(8,128)(2,1)}, bf16[256,4096]{1,0:T(8,128)(2,1)}, f32[256,128]{1,0:T(8,128)}, f32[256,128]{1,0:T(8,128)}, bf16[64,256]{1,0:T(8,128)(2,1)}) custom-call(bf16[256,4096]{1,0:T(8,128)(2,1)} %x_ref.5, bf16[256,4096]{1,0:T(8,128)(2,1)} %g_ref.5, bf16[256,4096]{1,0:T(8,128)(2,1)} %get-tuple-element.34.ymix_ref, ...), custom_call_target="tpu_custom_call" | custom-call | flops 8000000000 | bytes 16000000 | tf_op jit(solution)/shard_map/finish/pallas_call | solution.py:480
  116.9 0.0 all-to-all-done.2
  116.9 0.2 reduce_sum.9
  117.1 0.6 fusion
Async XLA Ops:
  63.1 35.2 %all-to-all-start.1 = ((bf16[128,64,128]{2,1,0:T(8,128)(2,1)}), bf16[128,64,128]{2,1,0:T(8,128)(2,1)}, u32[]{:S(2)}, u32[]{:S(2)}) async-start(bf16[128,64,128]{2,1,0:T(8,128)(2,1)} %scan.1), calls=%async_computation.1 | async-start | bytes 4194304 | tf_op jit(solution)/shard_map/all_to_all | solution.py:519
  102.9 14.0 %all-to-all-start.2 = ((f32[128,1,128]{2,1,0:T(1,128)}), f32[128,1,128]{2,1,0:T(1,128)S(1)}, u32[]{:S(2)}, u32[]{:S(2)}) async-start(f32[128,1,128]{2,1,0:T(1,128)} %bitcast.12), calls=%async_computation.2 | async-start | bytes 131072 | tf_op jit(solution)/shard_map/all_to_all | solution.py:521

commit v4 on v3

--- a/solution.py
+++ b/solution.py
@@ -305,7 +305,28 @@
     )(x, g, b, c, seg, skip, cum2, half)
 
 
-def scan_kernel(pay_ref, out_ref):
+def scan_kernel(pay_ref, out_ref, matrix_ref):
+    step = pl.program_id(0)
+
+    @pl.when(step == 0)
+    def _():
+        prepare(pay_ref, matrix_ref)
+
+    lower = iota((PARTS, 256), 1) & (128 - 1) < DIM
+    first = step * 16
+    matrix = matrix_ref[first // PIECE]
+    for k in range(0, 16, 16):
+        block = jnp.swapaxes(pay_ref[:, pl.ds(pl.multiple_of(first + k, 16), 16), :], 0, 1)
+        done = []
+        for i in range(0, 16, 2):
+            rows = jnp.concatenate([block[i], block[i + 1]], axis=1)
+            both = dot(matrix, rows)
+            pair = jnp.where(lower, both[:PARTS], both[PARTS:]).astype(BF16)
+            done += [pair[:, :128], pair[:, 128:]]
+        out_ref[:, k : k + 16, :] = jnp.swapaxes(jnp.stack(done), 0, 1)
+
+
+def prepare(pay_ref, matrix_ref):
     square = (PARTS, PARTS)
     notes = jnp.swapaxes(pay_ref[:, CARRY:, :].astype(F32), 0, 1)
     high, mid, low, first, last = (notes[k] for k in range(5))
@@ -322,25 +343,18 @@
         backward.append(carry.T.astype(BF16))
     forward = jnp.concatenate(forward, axis=0)
     backward = jnp.concatenate(backward, axis=0)
-    lower = iota((PARTS, 256), 1) & (128 - 1) < DIM
-
-    for k in range(0, CARRY, 16):
-        block = jnp.swapaxes(pay_ref[:, k : k + 16, :], 0, 1)
-        done = []
-        for i in range(0, 16, 2):
-            rows = jnp.concatenate([block[i], block[i + 1]], axis=1)
-            both = dot(forward if k < PIECE else backward, rows)
-            pair = jnp.where(lower, both[:PARTS], both[PARTS:]).astype(BF16)
-            done += [pair[:, :128], pair[:, 128:]]
-        out_ref[:, k : k + 16, :] = jnp.swapaxes(jnp.stack(done), 0, 1)
+    matrix_ref[0] = forward
+    matrix_ref[1] = backward
 
 
 def scan(pay):
     return pl.pallas_call(
         scan_kernel,
         out_shape=like((PARTS, CARRY, 128), BF16),
-        in_specs=[pl.BlockSpec(memory_space=pltpu.VMEM)],
-        out_specs=pl.BlockSpec(memory_space=pltpu.VMEM),
+        grid=(4,),
+        in_specs=[whole(PARTS, CARRY + META, 128)],
+        out_specs=pl.BlockSpec((PARTS, CARRY // 4, 128), lambda i: (0, i, 0)),
+        scratch_shapes=[pltpu.VMEM((2, 2 * PARTS, PARTS), BF16)],
         compiler_params=params(16),
         cost_estimate=cost(5 * 10**8, 5 * 10**6, 10**5),
         name="scan",
@@ -419,7 +433,7 @@
     x_ref, g_ref, ymix_ref, dxmix_ref, state_ref, b_ref, c_ref, half_ref, dbmix_ref, dcmix_ref,
     raw_ref, rate_ref, scal_ref, cpart_ref, ddecay_ref, ddt_ref,
     y_ref, dx_ref, db_ref, dc_ref, raw_grad_ref,
-    dstart_ref, dweight_ref,
+    terms_ref,
 ):
     step = pl.program_id(0)
 
@@ -427,8 +441,7 @@
     def _():
         db_ref[...] = dbmix_ref[...]
         dc_ref[...] = dcmix_ref[...]
-        dstart_ref[...] = jnp.zeros_like(dstart_ref)
-        dweight_ref[...] = jnp.zeros_like(dweight_ref)
+        terms_ref[...] = jnp.zeros_like(terms_ref)
 
     h_low, lam_low = carried(state_ref)
     g_scaled, x_weighted, start_terms, weight_terms = [], [], [], []
@@ -451,23 +464,24 @@
     dc_ref[...] += dot_nt(jnp.concatenate(g_scaled, axis=1), h_low)
     db_ref[...] += dot_nt(jnp.concatenate(x_weighted, axis=1), lam_low)
     gather = gather_heads(step * (FINISH_LANES // DIM), FINISH_LANES, FINISH_LANES)
-    dstart_ref[...] += dot(jnp.concatenate(start_terms, axis=1), gather)
-    dweight_ref[...] += dot(jnp.concatenate(weight_terms, axis=1), gather)
+    none = jnp.zeros_like(gather)
+    terms = dot(jnp.concatenate(start_terms, axis=1), jnp.concatenate([gather, none], axis=1))
+    terms += dot(jnp.concatenate(weight_terms, axis=1), jnp.concatenate([none, gather], axis=1))
+    terms_ref[...] += terms
 
     @pl.when(step == WIDTH // FINISH_LANES - 1)
     def _():
         end, weight, start = (scal_ref[k] for k in range(3))
-        d_weight = dweight_ref[...].T
+        all_terms = terms_ref[...].T
+        d_weight = all_terms[HEADS:]
         used = d_weight * weight
-        d_cum = cpart_ref[...] + dstart_ref[...].T - used
-        at_last = iota((HEADS, BLOCK), 1) == BLOCK - 1
+        d_cum = cpart_ref[...] + all_terms[:HEADS] - used
         d_total = jnp.sum(used, axis=1, keepdims=True)
         d_total = d_total + ddecay_ref[:, :1] * start[:, BLOCK - 1 :]
-        d_cum = d_cum + jnp.where(at_last, d_total, 0.0)
         square = (BLOCK, BLOCK)
         onward = ones_where(iota(square, 0) >= iota(square, 1))
-        high, mid, low = split3(d_cum)
-        d_log = dot(high, onward) + dot(mid, onward) + dot(low, onward)
+        logs = dot(jnp.concatenate(split3(d_cum), axis=0), onward)
+        d_log = logs[:HEADS] + logs[HEADS : 2 * HEADS] + logs[2 * HEADS :] + d_total
         d_dt = ddt_ref[...] + d_weight * end - rate_ref[:, :1] * d_log
         raw = raw_ref[...].astype(F32)
         raw_grad_ref[...] = (d_dt / (1.0 + jnp.exp(-raw))).astype(BF16)
@@ -495,7 +509,7 @@
             like((BLOCK, WIDTH), BF16), like((BLOCK, WIDTH), BF16),
             like((BLOCK, STATE)), like((BLOCK, STATE)), like((HEADS, BLOCK), BF16),
         ],
-        scratch_shapes=[pltpu.VMEM((BLOCK, HEADS), F32)] * 2,
+        scratch_shapes=[pltpu.VMEM((BLOCK, 2 * HEADS), F32)],
         compiler_params=params(),
         cost_estimate=cost(8 * 10**9, 16 * 10**6, 10**5),
         name="finish",

time: 118 us -> 118 us (level)
  no operation moved by 1% of the time
where the time goes in v4:
time: 118 us; the launch traced here: 117 us
  blocking collectives  52.9 us (45%)
  Pallas kernels  44.4 us (38%)
  waiting for transfers between devices  9.41 us (8%)
  starting transfers between devices  8.63 us (7%)
    all_to_all x1, blocking collectives, body(): pay = lax.all_to_all(pay, everyone, 0, 0, tiled=True)  44 us
    pallas_call x1, Pallas kernels, mix(): pl.pallas_call(mix_kernel, grid=(WIDTH // MIX_LANES,), in_specs=[wide(MIX...  20.9 us
    pallas_call x1, Pallas kernels, finish(): pl.pallas_call(finish_kernel, grid=(WIDTH // lanes,), in_specs=[wide(lane...  10 us
    all_to_all x1, waiting for transfers between devices, body(): state = lax.all_to_all(scan(pay), everyone, 0, 0, tiled=True)  9.41 us
    all_gather x1, blocking collectives, body(): gains = lax.all_gather(jnp.stack([a_log, d_skip]), 'head', tiled=True)  8.89 us
    pallas_call x1, Pallas kernels, states(): pl.pallas_call(states_kernel, grid=(WIDTH // STATES_LANES,), in_specs=[pl...  5.34 us
    all_to_all x1, starting transfers between devices, body(): state = lax.all_to_all(scan(pay), everyone, 0, 0, tiled=True)  4.81 us
    pallas_call x1, Pallas kernels, gradient_sums(): pl.pallas_call(sums_kernel, grid=(WIDTH // SUMS_LANES,), in_specs=[moment...  4.61 us
  transfers between devices with their start and end apart: 2, of which 1 were waited for; matrix products, arithmetic and copies ran while one was open for 0% of the time, Pallas kernels for 26%

profile of v4, /device:TPU:1, one launch (start us, length us, event | category | flops | bytes accessed | tf_op | source)
XLA Modules:
  0.0 117.4 jit_solution(18258523693801474156)
XLA Ops:
  0.6 0.7 maximum_bitcast_fusion
  1.3 8.9 %all-gather = f32[4,2,16]{2,1,0:T(2,128)} all-gather(f32[1,2,16]{2,1,0:T(2,128)S(1)} %maximum_bitcast_fusion), channel_id=1, replica_groups=mesh['head'=4,'seq'=32] {'head'}, dimensions={0}, use_global_device_ids=true | all-gather | bytes 640 | tf_op jit(solution)/shard_map/all_gather | solution.py:524
  10.2 5.3 %states.1 = (bf16[128,72,128]{2,1,0:T(8,128)(2,1)}, f32[4,64,256]{2,1,0:T(8,128)}, f32[64,256]{1,0:T(8,128)}, bf16[5,256,128]{2,1,0:T(8,128)(2,1)}, f32[64,128]{...) custom-call(s32[1]{0:T(128)} %bitcast.place_ref, bf16[64,256]{1,0:T(8,128)(2,1)} %bitcast.13, f32[8,16]{1,0:T(8,128)} %bitcast.15, ...), custom_call_target="tpu_custom_call" | custom-call | flops 1000000000 | bytes 8000000 | tf_op jit(solution)/shard_map/states/pallas_call | solution.py:166
  15.6 44.0 %all_to_all.15.pay_ref = bf16[128,72,128]{2,1,0:T(8,128)(2,1)S(1)} all-to-all(bf16[128,72,128]{2,1,0:T(8,128)(2,1)} %get-tuple-element.36), channel_id=1, replica_groups=mesh['head'=4,'seq'=32] {'seq','head'}, dimensions={0} | all-to-all | bytes 4718592 | tf_op jit(solution)/shard_map/all_to_all | solution.py:529
  59.6 3.4 %scan.1 = bf16[128,64,128]{2,1,0:T(8,128)(2,1)} custom-call(bf16[128,72,128]{2,1,0:T(8,128)(2,1)S(1)} %all_to_all.15.pay_ref), custom_call_target="tpu_custom_call" | custom-call | flops 500000000 | bytes 5000000 | tf_op jit(solution)/shard_map/scan/pallas_call | solution.py:351
  63.0 4.8 %all-to-all-start.1 = ((bf16[128,64,128]{2,1,0:T(8,128)(2,1)}), bf16[128,64,128]{2,1,0:T(8,128)(2,1)}, u32[]{:S(2)}, u32[]{:S(2)}) async-start(bf16[128,64,128]{2,1,0:T(8,128)(2,1)} %scan.1), calls=%async_computation.1 | async-start | bytes 4194304 | tf_op jit(solution)/shard_map/all_to_all | solution.py:533
  67.8 20.9 %mix.1 = (bf16[256,4096]{1,0:T(8,128)(2,1)}, bf16[256,4096]{1,0:T(8,128)(2,1)}, f32[64,256]{1,0:T(8,128)}, f32[64,256]{1,0:T(8,128)}, f32[256,128]{1,0:T(8,128)}...) custom-call(bf16[256,4096]{1,0:T(8,128)(2,1)} %x_ref.5, ...), custom_call_target="tpu_custom_call" | custom-call | flops 20000000000 | bytes 9000000 | tf_op jit(solution)/shard_map/mix/pallas_call | solution.py:277
  88.8 9.4 %all-to-all-done.1.state_ref = bf16[128,64,128]{2,1,0:T(8,128)(2,1)} async-done(((bf16[128,64,128]{2,1,0:T(8,128)(2,1)}), bf16[128,64,128]{2,1,0:T(8,128)(2,1)}, u32[]{:S(2)}, u32[]{:S(2)}) %all-to-all-start.1) | async-done | bytes 2097184 | tf_op jit(solution)/shard_map/all_to_all | solution.py:533
  98.2 4.6 %gradient_sums.1 = (f32[64,128]{1,0:T(8,128)}, f32[128,128]{1,0:T(8,128)}) custom-call(bf16[128,4096]{1,0:T(8,128)(2,1)} %get-tuple-element.42.start_mom_ref, bf16[128,4096]{1,0:T(8,128)(2,1)} %get-tuple-element.43.end_mom_ref, bf16[128,64,128]{2,1,0:T(8,128)(2,1)} %all-to-all-done.1.state_ref, f32[4,64,256]{2,1,0:T(8,128)} %get-tuple-element.40.scal_ref, ...), custom_call_target="tpu_custom_call" | custom-call | flops 100000000 | bytes 4000000 | tf_op jit(solution)/shard_map/gradient_sums/pallas_call | solution.py:413
  102.8 3.8 %all-to-all-start.2 = ((f32[128,1,128]{2,1,0:T(1,128)}), f32[128,1,128]{2,1,0:T(1,128)S(1)}, u32[]{:S(2)}, u32[]{:S(2)}) async-start(f32[128,1,128]{2,1,0:T(1,128)} %bitcast.12), calls=%async_computation.2 | async-start | bytes 131072 | tf_op jit(solution)/shard_map/all_to_all | solution.py:535
  106.6 10.0 %finish.1 = (bf16[256,4096]{1,0:T(8,128)(2,1)}, bf16[256,4096]{1,0:T(8,128)(2,1)}, f32[256,128]{1,0:T(8,128)}, f32[256,128]{1,0:T(8,128)}, bf16[64,256]{1,0:T(8,128)(2,1)}) custom-call(bf16[256,4096]{1,0:T(8,128)(2,1)} %x_ref.5, bf16[256,4096]{1,0:T(8,128)(2,1)} %g_ref.5, bf16[256,4096]{1,0:T(8,128)(2,1)} %get-tuple-element.34.ymix_ref, ...), custom_call_target="tpu_custom_call" | custom-call | flops 8000000000 | bytes 16000000 | tf_op jit(solution)/shard_map/finish/pallas_call | solution.py:494
  116.6 0.0 all-to-all-done.2
  116.6 0.2 reduce_sum.9
  116.8 0.6 fusion
Async XLA Ops:
  63.0 35.2 %all-to-all-start.1 = ((bf16[128,64,128]{2,1,0:T(8,128)(2,1)}), bf16[128,64,128]{2,1,0:T(8,128)(2,1)}, u32[]{:S(2)}, u32[]{:S(2)}) async-start(bf16[128,64,128]{2,1,0:T(8,128)(2,1)} %scan.1), calls=%async_computation.1 | async-start | bytes 4194304 | tf_op jit(solution)/shard_map/all_to_all | solution.py:533
  102.8 13.9 %all-to-all-start.2 = ((f32[128,1,128]{2,1,0:T(1,128)}), f32[128,1,128]{2,1,0:T(1,128)S(1)}, u32[]{:S(2)}, u32[]{:S(2)}) async-start(f32[128,1,128]{2,1,0:T(1,128)} %bitcast.12), calls=%async_computation.2 | async-start | bytes 131072 | tf_op jit(solution)/shard_map/all_to_all | solution.py:535
